TPU v7x, 256 devices: a whole 4x4x8 slice. The times are simulated.
256 devices in a mesh: blk: 8 (over x_hi, y), grp: 32 (over x_lo, z, core).
Axes of the slice: x: 4 (x_hi: 2, x_lo: 2; x = x_hi * 2 + x_lo), y: 4, z: 8, core: 2. Of those that a mesh axis runs over, the one named last changes fastest.
Arguments:
- embeddings: bfloat16 [1024, 1024], P('blk'), may hold values from -8 to 8
- centroids: bfloat16 [524288, 1024], P(('blk', 'grp')), may hold values from -2 to 2
Outputs:
- centroid_sums: float32 [524288, 1024], P(('blk', 'grp'))
- centroid_mass: float32 [524288], P(('blk', 'grp'))
All inputs are finite; a program needn't handle non-finite values.
Results may differ from a plain program's by a relative error of at most 0.014.
Values may be sent and summed in bfloat16 or wider, within the bound.
No kernel may reach another device: no remote copies, remote signals or barrier semaphores. Data moves between devices by JAX's collectives and lax.ppermute only.
A program may use at most 128 MiB of HBM per device.

v0:
```python
import jax
import jax.numpy as jnp
from jax import lax
from jax.sharding import PartitionSpec as P

sharpness = 3.0


def shifted(value, axis, steps):
    count = lax.axis_size(axis)
    pairs = [(source, (source + steps) % count) for source in range(count)]
    return lax.ppermute(value, axis, pairs)


def merged(part, axis, combine):
    gathered = jax.tree.map(lambda a: lax.all_gather(a, axis), part)

    def take(source):
        return jax.tree.map(lambda a: lax.dynamic_index_in_dim(a, source, 0, False), gathered)

    return lax.fori_loop(
        1, lax.axis_size(axis), lambda source, state: combine(state, take(source)), take(0)
    )


def combine(first, second):
    highest = jnp.maximum(first[0], second[0])
    totals = first[1] * jnp.exp(first[0] - highest) + second[1] * jnp.exp(second[0] - highest)
    return (highest, totals)


def rotate(values):
    return shifted(values, "blk", 1)


def per_device(embeddings, centroids):
    group_count = lax.axis_size("blk")
    own_index = lax.axis_index("blk")
    row_count = embeddings.shape[0]
    squared = jnp.sum(jnp.square(centroids.astype(jnp.float32)), axis=1)

    def score_block(row_block):
        product = lax.dot_general(
            row_block, centroids, (((1,), (1,)), ((), ())), preferred_element_type=jnp.float32
        )
        return sharpness * (product - 0.5 * squared[None, :])

    gathered = None
    current = embeddings
    highs = jnp.zeros((group_count, row_count), jnp.float32)
    totals = jnp.zeros((group_count, row_count), jnp.float32)
    for position in range(group_count):
        row_block = current
        table_slot = (own_index - position) % group_count
        scores = score_block(row_block)
        highest = jnp.max(scores, axis=1)
        row_total = jnp.sum(jnp.exp(scores - highest[:, None]), axis=1)
        highest, row_total = merged((highest, row_total), "grp", combine)
        highs = highs.at[table_slot].set(highest)
        totals = totals.at[table_slot].set(row_total)
        if gathered is None and position + 1 < group_count:
            current = rotate(current)
    highs, totals = merged((highs, totals), "blk", combine)
    log_norm = highs + jnp.log(totals)
    weighted = jnp.zeros((centroids.shape[0], centroids.shape[1]), jnp.float32)
    total_mass = jnp.zeros((centroids.shape[0],), jnp.float32)
    for position in range(group_count):
        row_block = current
        table_slot = (own_index - (group_count - 1) - position) % group_count
        row_norm = lax.dynamic_index_in_dim(log_norm, table_slot, 0, keepdims=False)
        scores = score_block(row_block)
        weights = jnp.exp(scores - row_norm[:, None])
        total_mass = total_mass + jnp.sum(weights, axis=0)
        rounded = weights.astype(jnp.bfloat16)
        weighted = weighted + lax.dot_general(
            rounded, row_block, (((0,), (0,)), ((), ())), preferred_element_type=jnp.float32
        )
        if gathered is None and position + 1 < group_count:
            current = rotate(current)
    return (weighted, total_mass)


def solution(mesh):
    in_specs = (P("blk", None), P(("blk", "grp"), None))
    out_specs = (P(("blk", "grp"), None), P(("blk", "grp")))
    return jax.shard_map(
        per_device, mesh=mesh, in_specs=in_specs, out_specs=out_specs, check_vma=False
    )
```

profile of v0, /device:TPU:32, one launch (start us, length us, event | category | flops | bytes accessed | tf_op | source)
XLA Modules:
  0.0 792.3 jit_solution(10040128812373062609)
XLA Ops:
  0.6 1.7 collective-permute-start
  2.3 3.2 multiply_reduce_fusion
  5.7 1.6 fusion.77
  7.6 33.9 %all-gather.16 = f32[32,1,128]{2,1,0:T(1,128)S(1)} all-gather(f32[1,1,128]{2,1,0:T(1,128)S(1)} %bitcast.320), channel_id=2, replica_groups=mesh['blk'=8,'grp'=32] {'grp'}, dimensions={0}, use_global_device_ids=true | all-gather | bytes 16896 | tf_op jit(solution)/shard_map/all_gather | solution.py:16
  41.6 33.3 %all-gather.17 = f32[32,1,128]{2,1,0:T(1,128)S(1)} all-gather(f32[1,1,128]{2,1,0:T(1,128)S(1)} %bitcast.327), channel_id=3, replica_groups=mesh['blk'=8,'grp'=32] {'grp'}, dimensions={0}, use_global_device_ids=true | all-gather | bytes 16896 | tf_op jit(solution)/shard_map/all_gather | solution.py:16
  74.8 1.4 while.169
  78.7 3.8 fusion.78
  82.8 30.5 %all-gather.18 = f32[32,1,128]{2,1,0:T(1,128)S(1)} all-gather(f32[1,1,128]{2,1,0:T(1,128)S(1)} %bitcast.321), channel_id=4, replica_groups=mesh['blk'=8,'grp'=32] {'grp'}, dimensions={0}, use_global_device_ids=true | all-gather | bytes 16896 | tf_op jit(solution)/shard_map/all_gather | solution.py:16
  113.3 31.9 %all-gather.19 = f32[32,1,128]{2,1,0:T(1,128)S(1)} all-gather(f32[1,1,128]{2,1,0:T(1,128)S(1)} %bitcast.328), channel_id=5, replica_groups=mesh['blk'=8,'grp'=32] {'grp'}, dimensions={0}, use_global_device_ids=true | all-gather | bytes 16896 | tf_op jit(solution)/shard_map/all_gather | solution.py:16
  145.1 1.4 while.170
  146.5 1.7 collective-permute-start.1
  149.6 9.1 %collective-permute-done.1 = bf16[128,1024]{1,0:T(8,128)(2,1)S(1)} collective-permute-done((bf16[128,1024]{1,0:T(8,128)(2,1)S(1)}, bf16[128,1024]{1,0:T(8,128)(2,1)S(1)}, u32[]{:S(2)}, u32[]{:S(2)}) %collective-permute-start.1) | collective-permute-done | bytes 262176 | tf_op jit(solution)/shard_map/ppermute | solution.py:12
  158.7 3.8 fusion.79
  162.8 30.5 %all-gather.20 = f32[32,1,128]{2,1,0:T(1,128)S(1)} all-gather(f32[1,1,128]{2,1,0:T(1,128)S(1)} %bitcast.322), channel_id=6, replica_groups=mesh['blk'=8,'grp'=32] {'grp'}, dimensions={0}, use_global_device_ids=true | all-gather | bytes 16896 | tf_op jit(solution)/shard_map/all_gather | solution.py:16
  193.3 31.9 %all-gather.21 = f32[32,1,128]{2,1,0:T(1,128)S(1)} all-gather(f32[1,1,128]{2,1,0:T(1,128)S(1)} %bitcast.329), channel_id=7, replica_groups=mesh['blk'=8,'grp'=32] {'grp'}, dimensions={0}, use_global_device_ids=true | all-gather | bytes 16896 | tf_op jit(solution)/shard_map/all_gather | solution.py:16
  225.1 1.4 while.171
  227.9 10.8 %collective-permute-done.2 = bf16[128,1024]{1,0:T(8,128)(2,1)S(1)} collective-permute-done((bf16[128,1024]{1,0:T(8,128)(2,1)S(1)}, bf16[128,1024]{1,0:T(8,128)(2,1)S(1)}, u32[]{:S(2)}, u32[]{:S(2)}) %collective-permute-start.2) | collective-permute-done | bytes 262176 | tf_op jit(solution)/shard_map/ppermute | solution.py:12
  238.7 3.8 fusion.80
  242.8 30.5 %all-gather.22 = f32[32,1,128]{2,1,0:T(1,128)S(1)} all-gather(f32[1,1,128]{2,1,0:T(1,128)S(1)} %bitcast.323), channel_id=8, replica_groups=mesh['blk'=8,'grp'=32] {'grp'}, dimensions={0}, use_global_device_ids=true | all-gather | bytes 16896 | tf_op jit(solution)/shard_map/all_gather | solution.py:16
  273.3 31.9 %all-gather.23 = f32[32,1,128]{2,1,0:T(1,128)S(1)} all-gather(f32[1,1,128]{2,1,0:T(1,128)S(1)} %bitcast.330), channel_id=9, replica_groups=mesh['blk'=8,'grp'=32] {'grp'}, dimensions={0}, use_global_device_ids=true | all-gather | bytes 16896 | tf_op jit(solution)/shard_map/all_gather | solution.py:16
  305.1 1.4 while.172
  308.4 10.7 %collective-permute-done.3 = bf16[128,1024]{1,0:T(8,128)(2,1)S(1)} collective-permute-done((bf16[128,1024]{1,0:T(8,128)(2,1)S(1)}, bf16[128,1024]{1,0:T(8,128)(2,1)S(1)}, u32[]{:S(2)}, u32[]{:S(2)}) %collective-permute-start.3) | collective-permute-done | bytes 262176 | tf_op jit(solution)/shard_map/ppermute | solution.py:12
  319.2 3.8 fusion.81
  323.3 30.5 %all-gather.24 = f32[32,1,128]{2,1,0:T(1,128)S(1)} all-gather(f32[1,1,128]{2,1,0:T(1,128)S(1)} %bitcast.324), channel_id=10, replica_groups=mesh['blk'=8,'grp'=32] {'grp'}, dimensions={0}, use_global_device_ids=true | all-gather | bytes 16896 | tf_op jit(solution)/shard_map/all_gather | solution.py:16
  353.7 31.9 %all-gather.25 = f32[32,1,128]{2,1,0:T(1,128)S(1)} all-gather(f32[1,1,128]{2,1,0:T(1,128)S(1)} %bitcast.331), channel_id=11, replica_groups=mesh['blk'=8,'grp'=32] {'grp'}, dimensions={0}, use_global_device_ids=true | all-gather | bytes 16896 | tf_op jit(solution)/shard_map/all_gather | solution.py:16
  385.6 1.4 while.173
  388.4 10.7 %collective-permute-done.4 = bf16[128,1024]{1,0:T(8,128)(2,1)S(1)} collective-permute-done((bf16[128,1024]{1,0:T(8,128)(2,1)S(1)}, bf16[128,1024]{1,0:T(8,128)(2,1)S(1)}, u32[]{:S(2)}, u32[]{:S(2)}) %collective-permute-start.4) | collective-permute-done | bytes 262176 | tf_op jit(solution)/shard_map/ppermute | solution.py:12
  399.2 3.8 fusion.82
  403.3 30.5 %all-gather.26 = f32[32,1,128]{2,1,0:T(1,128)S(1)} all-gather(f32[1,1,128]{2,1,0:T(1,128)S(1)} %bitcast.325), channel_id=12, replica_groups=mesh['blk'=8,'grp'=32] {'grp'}, dimensions={0}, use_global_device_ids=true | all-gather | bytes 16896 | tf_op jit(solution)/shard_map/all_gather | solution.py:16
  433.7 31.9 %all-gather.27 = f32[32,1,128]{2,1,0:T(1,128)S(1)} all-gather(f32[1,1,128]{2,1,0:T(1,128)S(1)} %bitcast.332), channel_id=13, replica_groups=mesh['blk'=8,'grp'=32] {'grp'}, dimensions={0}, use_global_device_ids=true | all-gather | bytes 16896 | tf_op jit(solution)/shard_map/all_gather | solution.py:16
  465.6 1.4 while.174
  468.4 10.8 %collective-permute-done.5 = bf16[128,1024]{1,0:T(8,128)(2,1)S(1)} collective-permute-done((bf16[128,1024]{1,0:T(8,128)(2,1)S(1)}, bf16[128,1024]{1,0:T(8,128)(2,1)S(1)}, u32[]{:S(2)}, u32[]{:S(2)}) %collective-permute-start.5) | collective-permute-done | bytes 262176 | tf_op jit(solution)/shard_map/ppermute | solution.py:12
  479.2 3.8 fusion.83
  483.2 30.5 %all-gather.28 = f32[32,1,128]{2,1,0:T(1,128)S(1)} all-gather(f32[1,1,128]{2,1,0:T(1,128)S(1)} %bitcast.326), channel_id=14, replica_groups=mesh['blk'=8,'grp'=32] {'grp'}, dimensions={0}, use_global_device_ids=true | all-gather | bytes 16896 | tf_op jit(solution)/shard_map/all_gather | solution.py:16
  513.7 31.9 %all-gather.29 = f32[32,1,128]{2,1,0:T(1,128)S(1)} all-gather(f32[1,1,128]{2,1,0:T(1,128)S(1)} %bitcast.333), channel_id=15, replica_groups=mesh['blk'=8,'grp'=32] {'grp'}, dimensions={0}, use_global_device_ids=true | all-gather | bytes 16896 | tf_op jit(solution)/shard_map/all_gather | solution.py:16
  545.6 1.4 while.175
  548.5 10.6 %collective-permute-done.6 = bf16[128,1024]{1,0:T(8,128)(2,1)S(1)} collective-permute-done((bf16[128,1024]{1,0:T(8,128)(2,1)S(1)}, bf16[128,1024]{1,0:T(8,128)(2,1)S(1)}, u32[]{:S(2)}, u32[]{:S(2)}) %collective-permute-start.6) | collective-permute-done | bytes 262176 | tf_op jit(solution)/shard_map/ppermute | solution.py:12
  559.1 3.8 fusion.84
  563.2 30.5 %all-gather.31 = f32[32,1,128]{2,1,0:T(1,128)S(1)} all-gather(f32[1,1,128]{2,1,0:T(1,128)S(1)} %bitcast.334), channel_id=17, replica_groups=mesh['blk'=8,'grp'=32] {'grp'}, dimensions={0}, use_global_device_ids=true | all-gather | bytes 16896 | tf_op jit(solution)/shard_map/all_gather | solution.py:16
  593.7 31.9 %all-gather.30 = f32[32,1,128]{2,1,0:T(1,128)S(1)} all-gather(f32[1,1,128]{2,1,0:T(1,128)S(1)} %bitcast.319), channel_id=16, replica_groups=mesh['blk'=8,'grp'=32] {'grp'}, dimensions={0}, use_global_device_ids=true | all-gather | bytes 16896 | tf_op jit(solution)/shard_map/all_gather | solution.py:16
  625.6 1.4 while.176
  627.6 34.1 %all_gather.146 = f32[8,8,128]{2,1,0:T(8,128)S(1)} all-gather(f32[1,8,128]{2,1,0:T(8,128)S(1)} %scatter.65), channel_id=1, replica_groups=mesh['blk'=8,'grp'=32] {'blk'}, dimensions={0}, use_global_device_ids=true | all-gather | bytes 36864 | tf_op jit(solution)/shard_map/all_gather | solution.py:16
  662.3 34.1 %all_gather.149 = f32[8,8,128]{2,1,0:T(8,128)S(1)} all-gather(f32[1,8,128]{2,1,0:T(8,128)S(1)} %scatter.79), channel_id=1, replica_groups=mesh['blk'=8,'grp'=32] {'blk'}, dimensions={0}, use_global_device_ids=true | all-gather | bytes 36864 | tf_op jit(solution)/shard_map/all_gather | solution.py:16
  697.0 1.4 fusion.49
  698.6 8.4 %collective-permute-done.7 = bf16[128,1024]{1,0:T(8,128)(2,1)S(1)} collective-permute-done((bf16[128,1024]{1,0:T(8,128)(2,1)S(1)}, bf16[128,1024]{1,0:T(8,128)(2,1)S(1)}, u32[]{:S(2)}, u32[]{:S(2)}) %collective-permute-start.7) | collective-permute-done | bytes 262176 | tf_op jit(solution)/shard_map/ppermute | solution.py:12
  707.0 1.6 fusion.91
  709.8 7.1 collective-permute-done.8
  716.9 1.6 fusion.90
  718.5 4.5 fusion.60
  723.0 4.5 collective-permute-done.9
  727.5 1.6 fusion.89
  729.1 4.5 fusion.58
  733.6 5.6 collective-permute-done.10
  739.4 1.6 fusion.88
  741.0 4.5 fusion.56
  745.5 6.5 collective-permute-done.11
  752.0 1.6 fusion.87
  753.5 4.5 fusion.54
  758.0 3.9 collective-permute-done.12
  761.9 1.6 fusion.86
  763.5 4.7 fusion.52
  768.2 3.7 collective-permute-done.13
  771.9 1.6 fusion.85
  774.1 17.9 %add_add_fusion = f32[2048,1024]{1,0:T(8,128)} fusion(f32[2048,1024]{1,0:T(8,128)} %fusion.52, f32[2048,1024]{1,0:T(8,128)} %fusion.54, f32[2048,1024]{1,0:T(8,128)} %fusion.56, f32[2048,1024]{1,0:T(8,128)} %fusion.58, f32[2048,1024]{1,0:T(8,128)} %fusion.60, f32[2048,1024]{1,0:T(8,128)S(1)} %fusion.49, f32[2048,1024]{1,0:T(8,128)S(1)} %fusion.62, ...), kind=kOutput, calls=%fused_computation.53 | convolution fusion | flops 551550976 | bytes 67895296 | tf_op jit(solution)/shard_map/dot_general | solution.py:75
  (344 shorter events, 25.3 us)
Async XLA Ops:
  0.6 4.9 copy-start.2
  0.6 78.1 %collective-permute-start = (bf16[128,1024]{1,0:T(8,128)(2,1)}, bf16[128,1024]{1,0:T(8,128)(2,1)S(1)}, u32[]{:S(2)}, u32[]{:S(2)}) collective-permute-start(bf16[128,1024]{1,0:T(8,128)(2,1)} %param.52), channel_id=1, source_target_pairs={{0,32},{32,64},{64,96},{96,128},{128,160},{160,192},{192,224},{224... | collective-permute-start | bytes 786440 | tf_op jit(solution)/shard_map/ppermute | solution.py:12
  2.3 3.4 copy-start
  5.5 70.8 %copy-start.3 = (s32[2]{0:T(128)S(1)}, s32[2]{0:T(128)}, u32[]{:S(2)}) copy-start(s32[2]{0:T(128)} %constant.827.clone.1) | copy-start | bytes 28
  146.5 12.2 %collective-permute-start.1 = (bf16[128,1024]{1,0:T(8,128)(2,1)S(1)}, bf16[128,1024]{1,0:T(8,128)(2,1)S(1)}, u32[]{:S(2)}, u32[]{:S(2)}) collective-permute-start(bf16[128,1024]{1,0:T(8,128)(2,1)S(1)} %collective-permute-done), channel_id=1, source_target_pairs={{0,32},{32,64},{64,96},{96,128},{128,160},{160,192},{192,224},{224... | collective-permute-start | bytes 786440 | tf_op jit(solution)/shard_map/ppermute | solution.py:12
  226.5 12.2 %collective-permute-start.2 = (bf16[128,1024]{1,0:T(8,128)(2,1)S(1)}, bf16[128,1024]{1,0:T(8,128)(2,1)S(1)}, u32[]{:S(2)}, u32[]{:S(2)}) collective-permute-start(bf16[128,1024]{1,0:T(8,128)(2,1)S(1)} %collective-permute-done.1), channel_id=1, source_target_pairs={{0,32},{32,64},{64,96},{96,128},{128,160},{160,192},{192,224},{224... | collective-permute-start | bytes 786440 | tf_op jit(solution)/shard_map/ppermute | solution.py:12
  306.5 12.7 %collective-permute-start.3 = (bf16[128,1024]{1,0:T(8,128)(2,1)S(1)}, bf16[128,1024]{1,0:T(8,128)(2,1)S(1)}, u32[]{:S(2)}, u32[]{:S(2)}) collective-permute-start(bf16[128,1024]{1,0:T(8,128)(2,1)S(1)} %collective-permute-done.2), channel_id=1, source_target_pairs={{0,32},{32,64},{64,96},{96,128},{128,160},{160,192},{192,224},{224... | collective-permute-start | bytes 786440 | tf_op jit(solution)/shard_map/ppermute | solution.py:12
  387.0 12.2 %collective-permute-start.4 = (bf16[128,1024]{1,0:T(8,128)(2,1)S(1)}, bf16[128,1024]{1,0:T(8,128)(2,1)S(1)}, u32[]{:S(2)}, u32[]{:S(2)}) collective-permute-start(bf16[128,1024]{1,0:T(8,128)(2,1)S(1)} %collective-permute-done.3), channel_id=1, source_target_pairs={{0,32},{32,64},{64,96},{96,128},{128,160},{160,192},{192,224},{224... | collective-permute-start | bytes 786440 | tf_op jit(solution)/shard_map/ppermute | solution.py:12
  467.0 12.2 %collective-permute-start.5 = (bf16[128,1024]{1,0:T(8,128)(2,1)S(1)}, bf16[128,1024]{1,0:T(8,128)(2,1)S(1)}, u32[]{:S(2)}, u32[]{:S(2)}) collective-permute-start(bf16[128,1024]{1,0:T(8,128)(2,1)S(1)} %collective-permute-done.4), channel_id=1, source_target_pairs={{0,32},{32,64},{64,96},{96,128},{128,160},{160,192},{192,224},{224... | collective-permute-start | bytes 786440 | tf_op jit(solution)/shard_map/ppermute | solution.py:12
  546.9 12.2 %collective-permute-start.6 = (bf16[128,1024]{1,0:T(8,128)(2,1)S(1)}, bf16[128,1024]{1,0:T(8,128)(2,1)S(1)}, u32[]{:S(2)}, u32[]{:S(2)}) collective-permute-start(bf16[128,1024]{1,0:T(8,128)(2,1)S(1)} %collective-permute-done.5), channel_id=1, source_target_pairs={{0,32},{32,64},{64,96},{96,128},{128,160},{160,192},{192,224},{224... | collective-permute-start | bytes 786440 | tf_op jit(solution)/shard_map/ppermute | solution.py:12
  696.7 10.2 %collective-permute-start.7 = (bf16[128,1024]{1,0:T(8,128)(2,1)S(1)}, bf16[128,1024]{1,0:T(8,128)(2,1)S(1)}, u32[]{:S(2)}, u32[]{:S(2)}) collective-permute-start(bf16[128,1024]{1,0:T(8,128)(2,1)S(1)} %collective-permute-done.6), channel_id=1, source_target_pairs={{0,32},{32,64},{64,96},{96,128},{128,160},{160,192},{192,224},{224... | collective-permute-start | bytes 786440 | tf_op jit(solution)/shard_map/ppermute | solution.py:12
  697.0 10.0 %copy-start.1 = (bf16[2048,1024]{1,0:T(8,128)(2,1)S(1)}, bf16[2048,1024]{1,0:T(8,128)(2,1)}, u32[]{:S(2)}) copy-start(bf16[2048,1024]{1,0:T(8,128)(2,1)} %param.53) | copy-start | bytes 12582916
  707.0 10.0 %collective-permute-start.8 = (bf16[128,1024]{1,0:T(8,128)(2,1)S(1)}, bf16[128,1024]{1,0:T(8,128)(2,1)S(1)}, u32[]{:S(2)}, u32[]{:S(2)}) collective-permute-start(bf16[128,1024]{1,0:T(8,128)(2,1)S(1)} %collective-permute-done.7), channel_id=1, source_target_pairs={{0,32},{32,64},{64,96},{96,128},{128,160},{160,192},{192,224},{224... | collective-permute-start | bytes 786440 | tf_op jit(solution)/shard_map/ppermute | solution.py:12
  716.9 10.6 %collective-permute-start.9 = (bf16[128,1024]{1,0:T(8,128)(2,1)S(1)}, bf16[128,1024]{1,0:T(8,128)(2,1)S(1)}, u32[]{:S(2)}, u32[]{:S(2)}) collective-permute-start(bf16[128,1024]{1,0:T(8,128)(2,1)S(1)} %collective-permute-done.8), channel_id=1, source_target_pairs={{0,32},{32,64},{64,96},{96,128},{128,160},{160,192},{192,224},{224... | collective-permute-start | bytes 786440 | tf_op jit(solution)/shard_map/ppermute | solution.py:12
  727.5 11.7 %collective-permute-start.10 = (bf16[128,1024]{1,0:T(8,128)(2,1)S(1)}, bf16[128,1024]{1,0:T(8,128)(2,1)S(1)}, u32[]{:S(2)}, u32[]{:S(2)}) collective-permute-start(bf16[128,1024]{1,0:T(8,128)(2,1)S(1)} %collective-permute-done.9), channel_id=1, source_target_pairs={{0,32},{32,64},{64,96},{96,128},{128,160},{160,192},{192,224},{224... | collective-permute-start | bytes 786440 | tf_op jit(solution)/shard_map/ppermute | solution.py:12
  739.2 12.7 %collective-permute-start.11 = (bf16[128,1024]{1,0:T(8,128)(2,1)S(1)}, bf16[128,1024]{1,0:T(8,128)(2,1)S(1)}, u32[]{:S(2)}, u32[]{:S(2)}) collective-permute-start(bf16[128,1024]{1,0:T(8,128)(2,1)S(1)} %collective-permute-done.10), channel_id=1, source_target_pairs={{0,32},{32,64},{64,96},{96,128},{128,160},{160,192},{192,224},{224... | collective-permute-start | bytes 786440 | tf_op jit(solution)/shard_map/ppermute | solution.py:12
  751.9 10.0 %collective-permute-start.12 = (bf16[128,1024]{1,0:T(8,128)(2,1)S(1)}, bf16[128,1024]{1,0:T(8,128)(2,1)S(1)}, u32[]{:S(2)}, u32[]{:S(2)}) collective-permute-start(bf16[128,1024]{1,0:T(8,128)(2,1)S(1)} %collective-permute-done.11), channel_id=1, source_target_pairs={{0,32},{32,64},{64,96},{96,128},{128,160},{160,192},{192,224},{224... | collective-permute-start | bytes 786440 | tf_op jit(solution)/shard_map/ppermute | solution.py:12
  761.9 10.0 %collective-permute-start.13 = (bf16[128,1024]{1,0:T(8,128)(2,1)S(1)}, bf16[128,1024]{1,0:T(8,128)(2,1)S(1)}, u32[]{:S(2)}, u32[]{:S(2)}) collective-permute-start(bf16[128,1024]{1,0:T(8,128)(2,1)S(1)} %collective-permute-done.12), channel_id=1, source_target_pairs={{0,32},{32,64},{64,96},{96,128},{128,160},{160,192},{192,224},{224... | collective-permute-start | bytes 786440 | tf_op jit(solution)/shard_map/ppermute | solution.py:12
where the time goes:
time: 801 us; the launch traced here: 792 us
  blocking collectives  572 us (71%)
  waiting for transfers between devices  102 us (13%)
  matrix products  82.4 us (10%)
  other arithmetic  24.8 us (3%)
    all_gather x18, blocking collectives, merged(): gathered = jax.tree.map(lambda a: lax.all_gather(a, axis), part)  572 us
    ppermute x14, waiting for transfers between devices, shifted(): return lax.ppermute(value, axis, pairs)  102 us
    dot_general x8, matrix products, per_device(): lax.dot_general(rounded, row_block, (((0,), (0,)), ((), ())), preferred_e...  43.2 us
    dot_general x15, matrix products, score_block(): lax.dot_general(row_block, centroids, (((1,), (1,)), ((), ())), preferred...  39.2 us
  transfers between devices with their start and end apart: 14, of which 13 were waited for; matrix products, arithmetic and copies ran while one was open for 7% of the time, Pallas kernels for 0%

commit v1 on v0

v1 whole, which is shorter than its diff:
```python
import functools

import jax
import jax.numpy as jnp
from jax import lax
from jax.experimental import pallas as pl
from jax.experimental.pallas import tpu as pltpu
from jax.sharding import PartitionSpec as P

sharpness = 3.0
LOG2E = 1.4426950408889634
AXES = ("blk", "grp")
ROW_TILE = 256
CENT_TILE = 512
OUT_COLS = 256
OUT_ROWS = 1024
VMEM_LIMIT = 48 * 1024 * 1024

DEVICES = 256
X_HI, X_LO = 128, 16


def groups_by(key):
    groups = {}
    for device in range(DEVICES):
        groups.setdefault(key(device), []).append(device)
    return list(groups.values())


row_groups = groups_by(lambda d: (d % X_LO, (d // X_HI) ^ (d // X_LO % 2)))
plane_groups = groups_by(lambda d: d % X_LO)
column_groups = groups_by(lambda d: d // X_LO)


def in_vmem(value):
    return pltpu.with_memory_space_constraint(value, pltpu.VMEM)


def vmem_out(shape, dtype):
    return pltpu.VMEM(shape, dtype)


def score_kernel(first, *refs):
    if first:
        cents, rows, bias, probs, stats, scores = refs
    else:
        cents, rows, bias, earlier, probs, message, scores = refs
    cent_count, width = cents.shape
    row_count = rows.shape[0]
    cent_tiles = cent_count // CENT_TILE
    if first:
        def bias_step(i, carry):
            at = pl.ds(pl.multiple_of(i * CENT_TILE, CENT_TILE), CENT_TILE)
            block = cents[at, :].astype(jnp.float32)
            squared = jnp.sum(block * block, axis=1, keepdims=True)
            bias[at, :] = jnp.broadcast_to(squared * (-0.5 * sharpness * LOG2E), (CENT_TILE, 128))
            return carry
        lax.fori_loop(0, cent_tiles, bias_step, 0)
    found = []
    for j in range(row_count // ROW_TILE):
        row_block = rows[j * ROW_TILE:(j + 1) * ROW_TILE, :]

        def score_step(i, highest):
            at = pl.ds(pl.multiple_of(i * CENT_TILE, CENT_TILE), CENT_TILE)
            product = lax.dot_general(
                cents[at, :], row_block, (((1,), (1,)), ((), ())), preferred_element_type=jnp.float32
            )
            shift = jnp.concatenate([bias[at, :]] * (ROW_TILE // 128), axis=1)
            block = product * (sharpness * LOG2E) + shift
            scores[at, :] = block
            return jnp.maximum(highest, jnp.max(block.reshape(-1, 8, ROW_TILE), axis=0))

        highest = lax.fori_loop(
            0, cent_tiles, score_step, jnp.full((8, ROW_TILE), -jnp.inf, jnp.float32)
        )
        highest = jnp.max(highest, axis=0, keepdims=True)

        def exp_step(i, total):
            at = pl.ds(pl.multiple_of(i * CENT_TILE, CENT_TILE), CENT_TILE)
            block = jnp.exp2(scores[at, :] - highest)
            probs[at, j * ROW_TILE:(j + 1) * ROW_TILE] = block.astype(jnp.bfloat16)
            return total + jnp.sum(block.reshape(-1, 8, ROW_TILE), axis=0)

        total = lax.fori_loop(0, cent_tiles, exp_step, jnp.zeros((8, ROW_TILE), jnp.float32))
        found.append((highest, jnp.sum(total, axis=0, keepdims=True)))
    highest = jnp.concatenate([h for h, _ in found], axis=1)
    total = jnp.concatenate([t for _, t in found], axis=1)
    if first:
        stats[...] = jnp.concatenate([highest, total], axis=0)
    else:
        before = earlier[...]
        packed = jnp.concatenate([before[0:1], highest, before[1:2], total], axis=0)
        message[...] = jnp.broadcast_to(packed[None], message.shape)


def combined(received):
    parts = [received[k] for k in range(received.shape[0])]
    highest = functools.reduce(jnp.maximum, [p[0:2] for p in parts])
    total = functools.reduce(jnp.add, [p[2:4] * jnp.exp2(p[0:2] - highest) for p in parts])
    return highest, total


def ordered(core, pair):
    return jnp.where(core == 1, jnp.concatenate([pair[1:2], pair[0:1]], axis=0), pair)


def merge_kernel(core_ref, received, message):
    highest, total = combined(received)
    core = core_ref[0]
    packed = jnp.concatenate([ordered(core, highest), ordered(core, total)], axis=0)
    message[...] = jnp.broadcast_to(packed[None], message.shape)


def sum_kernel(core_ref, received, own, probs_a, probs_b, rows_a, rows_b, sums, mass, factors, weights):
    step, column = pl.program_id(0), pl.program_id(1)
    half = rows_a.shape[0]

    @pl.when(jnp.logical_and(step == 0, column == 0))
    def _():
        highest, total = combined(received)
        core = core_ref[0]
        highest, total = ordered(core, highest), ordered(core, total)
        factors[...] = jnp.exp2(own[0, 0:2] - highest) / total

    @pl.when(column == 0)
    def _():
        chunk = 128

        def weigh(i, carry):
            source = pl.ds(pl.multiple_of(step * OUT_ROWS + i * chunk, chunk), chunk)
            target = pl.ds(pl.multiple_of(i * chunk, chunk), chunk)
            wa = probs_a[source, :].astype(jnp.float32) * factors[0:1, :]
            wb = probs_b[source, :].astype(jnp.float32) * factors[1:2, :]
            weights[target, :half] = wa.astype(jnp.bfloat16)
            weights[target, half:] = wb.astype(jnp.bfloat16)
            part = wa + wb
            part = sum(part[:, k * 128:(k + 1) * 128] for k in range(half // 128))
            mass[pl.ds(step * (OUT_ROWS // chunk) + i, 1), :] = jnp.sum(part.T, axis=0, keepdims=True)
            return carry

        lax.fori_loop(0, OUT_ROWS // chunk, weigh, 0)

    at = pl.ds(pl.multiple_of(column * OUT_COLS, OUT_COLS), OUT_COLS)
    sums[...] = jnp.dot(
        weights[:, :half], rows_a[:, at], preferred_element_type=jnp.float32
    ) + jnp.dot(weights[:, half:], rows_b[:, at], preferred_element_type=jnp.float32)


def vmem_spec():
    return pl.BlockSpec(memory_space=pltpu.VMEM)


def params():
    return pltpu.CompilerParams(vmem_limit_bytes=VMEM_LIMIT)


def scored(cents, rows, bias=None, earlier=None):
    first = bias is None
    cent_count, half = cents.shape[0], rows.shape[0]
    probs = vmem_out((cent_count, half), jnp.bfloat16)
    if first:
        inputs = (cents, rows)
        outs = (vmem_out((cent_count, 128), jnp.float32), probs, vmem_out((2, half), jnp.float32))
    else:
        inputs = (cents, rows, bias, earlier)
        outs = (probs, vmem_out((len(plane_groups[0]), 4, half), jnp.float32))
    return pl.pallas_call(
        functools.partial(score_kernel, first),
        out_shape=outs,
        in_specs=[vmem_spec()] * len(inputs),
        out_specs=[vmem_spec()] * len(outs),
        scratch_shapes=[pltpu.VMEM((cent_count, ROW_TILE), jnp.float32)],
        compiler_params=params(),
    )(*[in_vmem(v) for v in inputs])


def merged(core, received):
    return pl.pallas_call(
        merge_kernel,
        out_shape=vmem_out((len(column_groups[0]),) + received.shape[1:], jnp.float32),
        in_specs=[pl.BlockSpec(memory_space=pltpu.SMEM), vmem_spec()],
        out_specs=vmem_spec(),
        compiler_params=params(),
    )(core, in_vmem(received))


def summed(core, received, own, probs_a, probs_b, rows_a, rows_b):
    cent_count, half = probs_a.shape
    width = rows_a.shape[1]
    inputs = (received, own, probs_a, probs_b, rows_a, rows_b)
    sums, mass = pl.pallas_call(
        sum_kernel,
        grid=(cent_count // OUT_ROWS, width // OUT_COLS),
        out_shape=(
            jax.ShapeDtypeStruct((cent_count, width), jnp.float32),
            jax.ShapeDtypeStruct((cent_count // 128, 128), jnp.float32),
        ),
        in_specs=[pl.BlockSpec(memory_space=pltpu.SMEM)] + [vmem_spec()] * len(inputs),
        out_specs=(
            pl.BlockSpec((OUT_ROWS, OUT_COLS), lambda i, j: (i, j)),
            vmem_spec(),
        ),
        scratch_shapes=[
            pltpu.VMEM((2, half), jnp.float32),
            pltpu.VMEM((OUT_ROWS, 2 * half), jnp.bfloat16),
        ],
        compiler_params=params(),
    )(core, *[in_vmem(v) for v in inputs])
    return sums, mass.reshape(-1)


def to_group(message, groups):
    return lax.all_to_all(message, AXES, 0, 0, tiled=True, axis_index_groups=groups)


def per_device(embeddings, centroids):
    core = lax.axis_index("grp") % 2
    core_ref = core.astype(jnp.int32).reshape(1)
    share = embeddings.shape[0] // 2
    mine = lax.dynamic_slice_in_dim(embeddings, core * share, share, 0)
    blocks = len(row_groups[0])
    rows_a = to_group(jnp.broadcast_to(mine[None], (blocks,) + mine.shape), row_groups)
    rows_a = rows_a.reshape(blocks * share, -1)
    rows_b = lax.ppermute(rows_a, AXES, [(d, d ^ 1) for d in range(DEVICES)])
    bias, probs_a, stats = scored(centroids, rows_a)
    probs_b, message = scored(centroids, rows_b, bias, stats)
    onward = merged(core_ref, to_group(message, plane_groups))
    received = to_group(onward, column_groups)
    return summed(core_ref, received, message, probs_a, probs_b, rows_a, rows_b)


def solution(mesh):
    in_specs = (P("blk", None), P(AXES, None))
    out_specs = (P(AXES, None), P(AXES))
    return jax.shard_map(
        per_device, mesh=mesh, in_specs=in_specs, out_specs=out_specs, check_vma=False
    )
```

time: 801 us -> 77.4 us (0.10)
  the two profiles are of different devices: /device:TPU:32 before, /device:TPU:1 now
where the time goes in v1:
time: 77.4 us; the launch traced here: 77.1 us
  blocking collectives  50.6 us (65%)
  Pallas kernels  20 us (26%)
  local copies, waits for them, and re-layouts  3.25 us (4%)
  starting transfers between devices  2.51 us (3%)
    all_to_all x3, blocking collectives, to_group(): lax.all_to_all(message, AXES, 0, 0, tiled=True, axis_index_groups=groups)  50.6 us
    pallas_call x2, Pallas kernels, scored(): pl.pallas_call(functools.partial(score_kernel, first), out_shape=outs, in...  10.2 us
    pallas_call x1, Pallas kernels, summed(): pl.pallas_call(sum_kernel, grid=(cent_count // OUT_ROWS, width // OUT_COL...  9.8 us
    unnamed x4, local copies, waits for them, and re-layouts  3.12 us
    ppermute x1, starting transfers between devices, per_device(): rows_b = lax.ppermute(rows_a, AXES, [(d, d ^ 1) for d in range(DEVICES)])  2.51 us
  transfers between devices with their start and end apart: 1, of which 0 were waited for; matrix products, arithmetic and copies ran while one was open for 0% of the time, Pallas kernels for 7%

profile of v1, /device:TPU:1, one launch (start us, length us, event | category | flops | bytes accessed | tf_op | source)
XLA Modules:
  0.0 77.1 jit_solution(7262934442786551403)
XLA Ops:
  0.6 0.0 copy-start
  0.7 0.9 %copy-done = bf16[128,1024]{1,0:T(8,128)(2,1)S(1)} copy-done((bf16[128,1024]{1,0:T(8,128)(2,1)S(1)}, bf16[128,1024]{1,0:T(8,128)(2,1)}, u32[]{:S(2)}) %copy-start) | copy-done | bytes 262168
  1.6 0.1 broadcast_in_dim.2
  1.7 22.3 %all_to_all.15 = bf16[8,64,1024]{2,1,0:T(8,128)(2,1)S(1)} all-to-all(bf16[8,64,1024]{2,1,0:T(8,128)(2,1)S(1)} %broadcast_in_dim.2), channel_id=1, replica_groups={{0,32,64,96,144,176,208,240},{1,33,65,97,145,177,209,241},{2,34,66,98,1..., dimensions={0} | all-to-all | bytes 2097152 | tf_op jit(solution)/shard_map/all_to_all | solution.py:213
  24.0 2.5 %collective-permute-start = (bf16[512,1024]{1,0:T(8,128)(2,1)S(1)}, bf16[512,1024]{1,0:T(8,128)(2,1)S(1)}, u32[]{:S(2)}, u32[]{:S(2)}) collective-permute-start(bf16[512,1024]{1,0:T(8,128)(2,1)S(1)} %bitcast.3), channel_id=1, source_target_pairs={{0,1},{1,0},{2,3},{3,2},{4,5},{5,4},{6,7},{7,6},{8,9},{9,8},{10,11... | collective-permute-start | bytes 3145736 | tf_op jit(solution)/shard_map/ppermute | solution.py:224
  26.5 0.0 copy-start.1
  26.5 2.2 %copy-done.1 = bf16[2048,1024]{1,0:T(8,128)(2,1)S(1)} copy-done((bf16[2048,1024]{1,0:T(8,128)(2,1)S(1)}, bf16[2048,1024]{1,0:T(8,128)(2,1)}, u32[]{:S(2)}) %copy-start.1) | copy-done | bytes 4194328
  28.7 5.6 %shard_map.41 = (f32[2048,128]{1,0:T(8,128)S(1)}, bf16[2048,512]{1,0:T(8,128)(2,1)S(1)}, f32[2,512]{1,0:T(2,128)S(1)}) custom-call(bf16[2048,1024]{1,0:T(8,128)(2,1)S(1)} %copy-done.1, bf16[512,1024]{1,0:T(8,128)(2,1)S(1)} %bitcast.4), custom_call_target="tpu_custom_call" | custom-call | tf_op jit(solution)/shard_map/pallas_call | solution.py:167
  34.3 0.0 collective-permute-done.refs_1_.rows_b
  34.4 4.6 %shard_map.42 = (bf16[2048,512]{1,0:T(8,128)(2,1)S(1)}, f32[16,4,512]{2,1,0:T(4,128)S(1)}) custom-call(bf16[2048,1024]{1,0:T(8,128)(2,1)S(1)} %copy-done.1, bf16[512,1024]{1,0:T(8,128)(2,1)S(1)} %collective-permute-done.refs_1_.rows_b, f32[2048,128]{1,0:T(8,128)S(1)} %get-tuple-element.9.refs_2_, f32[2,512]{1,0:T(2,128)S(1)} %get-tuple-element.10.refs_3_), custom_call_target="tpu_custom_call" | custom-call | tf_op jit(solution)/shard_map/pallas_call | solution.py:167
  38.9 9.9 %all_to_all.16.received = f32[16,4,512]{2,1,0:T(4,128)S(1)} all-to-all(f32[16,4,512]{2,1,0:T(4,128)S(1)} %get-tuple-element.11.own), channel_id=1, replica_groups={{0,16,32,48,64,80,96,112,128,144,160,176,192,208,224,240},{1,17,33,49,6..., dimensions={0} | all-to-all | bytes 262144 | tf_op jit(solution)/shard_map/all_to_all | solution.py:213
  48.8 0.1 shard_map.43
  48.9 18.5 %all_to_all.17.received = f32[16,4,512]{2,1,0:T(4,128)S(1)} all-to-all(f32[16,4,512]{2,1,0:T(4,128)S(1)} %shard_map.43), channel_id=1, replica_groups={{0,1,2,3,4,5,6,7,8,9,10,11,12,13,14,15},{16,17,18,19,20,21,22,23,24,25,..., dimensions={0} | all-to-all | bytes 262144 | tf_op jit(solution)/shard_map/all_to_all | solution.py:213
  67.3 9.8 %shard_map.44 = (f32[2048,1024]{1,0:T(8,128)}, f32[16,128]{1,0:T(8,128)}) custom-call(s32[1]{0:T(128)} %bitcast.core_ref, f32[16,4,512]{2,1,0:T(4,128)S(1)} %all_to_all.17.received, f32[16,4,512]{2,1,0:T(4,128)S(1)} %get-tuple-element.11.own, bf16[2048,512]{1,0:T(8,128)(2,1)S(1)} %get-tuple-element.12.probs_a, ...), custom_call_target="tpu_custom_call" | custom-call | tf_op jit(solution)/shard_map/pallas_call | solution.py:191
  (1 shorter events, 0.0 us)
Async XLA Ops:
  0.6 1.0 %copy-start = (bf16[128,1024]{1,0:T(8,128)(2,1)S(1)}, bf16[128,1024]{1,0:T(8,128)(2,1)}, u32[]{:S(2)}) copy-start(bf16[128,1024]{1,0:T(8,128)(2,1)} %param.2) | copy-start | bytes 786436
  24.0 10.3 %collective-permute-start = (bf16[512,1024]{1,0:T(8,128)(2,1)S(1)}, bf16[512,1024]{1,0:T(8,128)(2,1)S(1)}, u32[]{:S(2)}, u32[]{:S(2)}) collective-permute-start(bf16[512,1024]{1,0:T(8,128)(2,1)S(1)} %bitcast.3), channel_id=1, source_target_pairs={{0,1},{1,0},{2,3},{3,2},{4,5},{5,4},{6,7},{7,6},{8,9},{9,8},{10,11... | collective-permute-start | bytes 3145736 | tf_op jit(solution)/shard_map/ppermute | solution.py:224
  26.5 2.2 %copy-start.1 = (bf16[2048,1024]{1,0:T(8,128)(2,1)S(1)}, bf16[2048,1024]{1,0:T(8,128)(2,1)}, u32[]{:S(2)}) copy-start(bf16[2048,1024]{1,0:T(8,128)(2,1)} %refs_0_.3) | copy-start | bytes 12582916

commit v2 on v0

v2 whole, which is shorter than its diff:
```python
import functools

import jax
import jax.numpy as jnp
from jax import lax
from jax.experimental import pallas as pl
from jax.experimental.pallas import tpu as pltpu
from jax.sharding import PartitionSpec as P

sharpness = 3.0
LOG2E = 1.4426950408889634
SCALE = sharpness * LOG2E
AXES = ("blk", "grp")
LANES = 128
ROW_TILE = 256
CENT_TILE = 256
OUT_COLS = 512
OUT_ROWS = 256
MIB = 1024 * 1024
ARRIVALS = ((0, 256), (256, 256), (512, 512), (1024, 512), (1536, 512))

DEVICES = 256
X_HI, X_LO = 128, 16


def groups_by(key):
    groups = {}
    for device in range(DEVICES):
        groups.setdefault(key(device), []).append(device)
    return list(groups.values())


row_groups = groups_by(lambda d: (d % X_LO, (d // X_HI) ^ (d // X_LO % 2)))
plane_groups = groups_by(lambda d: d % X_LO)
column_groups = groups_by(lambda d: d // X_LO)


def in_vmem(value):
    return pltpu.with_memory_space_constraint(value, pltpu.VMEM)


def vmem_spec():
    return pl.BlockSpec(memory_space=pltpu.VMEM)


def part(i, size):
    return slice(i * size, (i + 1) * size)


def products(cents, rows, i, chunk):
    return lax.dot_general(
        cents[part(i, CENT_TILE), :],
        rows[part(chunk, ROW_TILE), :],
        (((1,), (1,)), ((), ())),
        preferred_element_type=jnp.float32,
    )


def shifted(block, bias):
    return block * SCALE + jnp.concatenate([bias] * (ROW_TILE // LANES), axis=1)


def fold(combine, block):
    return combine(block.reshape(-1, 8, block.shape[-1]), axis=0)


def no_highest():
    return jnp.full((8, ROW_TILE), -jnp.inf, jnp.float32)


def no_total():
    return jnp.zeros((8, ROW_TILE), jnp.float32)


def top(highest):
    return jnp.max(highest, axis=0, keepdims=True)


def whole(total):
    return jnp.sum(total, axis=0, keepdims=True)


def stacked(parts):
    return jnp.concatenate(
        [p[:, part(k, LANES)] for p in parts for k in range(p.shape[1] // LANES)], axis=0
    )


def exponentials(scores, highest, probs, i, column):
    block = jnp.exp2(scores[part(i, CENT_TILE), :] - highest)
    probs[part(i, CENT_TILE), part(column, ROW_TILE)] = block.astype(jnp.bfloat16)
    return fold(jnp.sum, block)


def first_kernel(source, rows, cents, bias, highs, scores_a, scores_b, arrived):
    copies = []
    for k, (start, size) in enumerate(ARRIVALS):
        at = pl.ds(start, size)
        copy = pltpu.make_async_copy(source.at[at, :], cents.at[at, :], arrived.at[k])
        copy.start()
        copies.append(copy)
    highest = [no_highest(), no_highest()]
    for copy, (start, size) in zip(copies, ARRIVALS):
        copy.wait()
        for i in range(start // CENT_TILE, (start + size) // CENT_TILE):
            block = cents[part(i, CENT_TILE), :].astype(jnp.float32)
            squared = jnp.sum(block * block, axis=1, keepdims=True)
            shift = jnp.broadcast_to(squared * (-0.5 * SCALE), (CENT_TILE, LANES))
            bias[part(i, CENT_TILE), :] = shift
            for chunk, scores in enumerate((scores_a, scores_b)):
                block = shifted(products(cents, rows, i, chunk), shift)
                scores[part(i, CENT_TILE), :] = block
                highest[chunk] = jnp.maximum(highest[chunk], fold(jnp.max, block))
    highs[...] = jnp.concatenate([top(h) for h in highest], axis=0)


def second_kernel(
    cents, rows, bias, highs, scores_a, scores_b, probs, own, message, scores_c, scores_d
):
    tiles = cents.shape[0] // CENT_TILE

    def step(chunk, scores, known):
        highest, totals = no_highest(), [no_total() for _ in known]
        for i in range(tiles):
            block = shifted(products(cents, rows, i, chunk), bias[part(i, CENT_TILE), :])
            scores[part(i, CENT_TILE), :] = block
            highest = jnp.maximum(highest, fold(jnp.max, block))
            for k, (before, high, column) in enumerate(known):
                totals[k] = totals[k] + exponentials(before, high, probs, i, column)
        return top(highest), [whole(t) for t in totals]

    highest_a, highest_b = highs[0:1, :], highs[1:2, :]
    highest_c, (total_a, total_b) = step(
        0, scores_c, [(scores_a, highest_a, 0), (scores_b, highest_b, 1)]
    )
    highest_d, (total_c,) = step(1, scores_d, [(scores_c, highest_c, 2)])
    total = no_total()
    for i in range(tiles):
        total = total + exponentials(scores_d, highest_d, probs, i, 3)
    highest = stacked([highest_a, highest_b, highest_c, highest_d])
    total = stacked([total_a, total_b, total_c, whole(total)])
    own[...] = highest
    message[...] = jnp.broadcast_to((highest + jnp.log(total) * LOG2E)[None], message.shape)


def combined(received):
    parts = [received[k] for k in range(received.shape[0])]
    highest = functools.reduce(jnp.maximum, parts)
    total = functools.reduce(jnp.add, [jnp.exp2(p - highest) for p in parts])
    return highest, total


def ordered(core, rows):
    half = rows.shape[0] // 2
    return jnp.where(core == 1, jnp.concatenate([rows[half:], rows[:half]], axis=0), rows)


def merge_kernel(core, received, message):
    highest, total = combined(received)
    merged = ordered(core[0], highest + jnp.log(total) * LOG2E)
    message[...] = jnp.broadcast_to(merged[None], message.shape)


def sum_kernel(
    core, received, own, probs, rows_a, rows_b,
    sums, mass, scaled, out, masses, sent, mass_sent,
):
    cent_count, width = out.shape
    half = rows_a.shape[0]
    highest, total = combined(received)
    factors = jnp.exp2(own[...] - ordered(core[0], highest)) / ordered(core[0], total)
    pieces = [(j, i) for j in range(width // OUT_COLS) for i in range(cent_count // OUT_ROWS)]
    tiles = cent_count // LANES
    copies = []
    for step, (j, i) in enumerate(pieces):
        columns = part(j, OUT_COLS)
        if i == 0:
            for k in range(2 * half // LANES):
                rows = (rows_a, rows_b)[k * LANES // half]
                factor = jnp.broadcast_to(factors[k:k + 1, :], (LANES, LANES)).T
                block = rows[part(k % (half // LANES), LANES), columns].astype(jnp.float32)
                block = block * jnp.concatenate([factor] * (OUT_COLS // LANES), axis=1)
                scaled[part(k, LANES), columns] = block.astype(jnp.bfloat16)
        at = part(i, OUT_ROWS)
        out[at, columns] = jnp.dot(
            probs[at, :], scaled[:, columns], preferred_element_type=jnp.float32
        )
        copy = pltpu.make_async_copy(out.at[at, columns], sums.at[at, columns], sent.at[step])
        copy.start()
        copies.append(copy)
        for k in range(tiles * step // (len(pieces) - 2), min(tiles, tiles * (step + 1) // (len(pieces) - 2))):
            at = part(k, LANES)
            lanes = 0.0
            for c in range(2 * half // LANES):
                block = probs[at, part(c, LANES)].astype(jnp.float32)
                lanes = lanes + block * factors[c:c + 1, :]
            masses[k:k + 1, :] = jnp.sum(lanes.T, axis=0, keepdims=True)
        if step == len(pieces) - 2:
            copy = pltpu.make_async_copy(masses, mass, mass_sent.at[0])
            copy.start()
            copies.append(copy)
    for copy in copies:
        copy.wait()


def call(kernel, inputs, in_specs, outs, out_specs, scratch, limit):
    return pl.pallas_call(
        kernel,
        out_shape=outs,
        in_specs=in_specs,
        out_specs=out_specs,
        scratch_shapes=scratch,
        compiler_params=pltpu.CompilerParams(vmem_limit_bytes=limit),
    )(*inputs)


def first_scores(centroids, rows):
    count, width = centroids.shape
    outs = (
        pltpu.VMEM((count, width), centroids.dtype),
        pltpu.VMEM((count, LANES), jnp.float32),
        pltpu.VMEM((2, ROW_TILE), jnp.float32),
        pltpu.VMEM((count, ROW_TILE), jnp.float32),
        pltpu.VMEM((count, ROW_TILE), jnp.float32),
    )
    scratch = [pltpu.SemaphoreType.DMA((len(ARRIVALS),))]
    in_specs = [pl.BlockSpec(memory_space=pltpu.HBM), vmem_spec()]
    inputs = (pltpu.with_memory_space_constraint(centroids, pltpu.HBM), in_vmem(rows))
    return call(first_kernel, inputs, in_specs, outs, [vmem_spec()] * len(outs), scratch, 12 * MIB)


def second_scores(cents, rows, bias, highs, scores_a, scores_b):
    count = cents.shape[0]
    row_tiles = 4 * ROW_TILE // LANES
    outs = (
        pltpu.VMEM((count, 4 * ROW_TILE), jnp.bfloat16),
        pltpu.VMEM((row_tiles, LANES), jnp.float32),
        pltpu.VMEM((len(plane_groups[0]), row_tiles, LANES), jnp.float32),
    )
    inputs = [in_vmem(v) for v in (cents, rows, bias, highs, scores_a, scores_b)]
    scratch = [pltpu.VMEM((count, ROW_TILE), jnp.float32)] * 2
    return call(
        second_kernel, inputs, [vmem_spec()] * len(inputs), outs, [vmem_spec()] * len(outs), scratch, 12 * MIB
    )


def merged(core, received):
    outs = pltpu.VMEM((len(column_groups[0]),) + received.shape[1:], jnp.float32)
    in_specs = [pl.BlockSpec(memory_space=pltpu.SMEM), vmem_spec()]
    return call(merge_kernel, (core, in_vmem(received)), in_specs, outs, vmem_spec(), [], 4 * MIB)


def summed(core, received, own, probs, rows_a, rows_b):
    count, width = probs.shape[0], rows_a.shape[1]
    inputs = [in_vmem(v) for v in (received, own, probs, rows_a, rows_b)]
    outs = (
        jax.ShapeDtypeStruct((count, width), jnp.float32),
        jax.ShapeDtypeStruct((count // LANES, LANES), jnp.float32),
    )
    scratch = [
        pltpu.VMEM((2 * rows_a.shape[0], width), jnp.bfloat16),
        pltpu.VMEM((count, width), jnp.float32),
        pltpu.VMEM((count // LANES, LANES), jnp.float32),
        pltpu.SemaphoreType.DMA(((count // OUT_ROWS) * (width // OUT_COLS),)),
        pltpu.SemaphoreType.DMA((1,)),
    ]
    in_specs = [pl.BlockSpec(memory_space=pltpu.SMEM)] + [vmem_spec()] * len(inputs)
    sums, mass = call(
        sum_kernel, [core] + inputs, in_specs, outs, [pl.BlockSpec(memory_space=pl.ANY)] * 2, scratch, 16 * MIB
    )
    return sums, mass.reshape(-1)


def to_group(message, groups):
    return lax.all_to_all(message, AXES, 0, 0, tiled=True, axis_index_groups=groups)


def per_device(embeddings, centroids):
    core = lax.axis_index("grp") % 2
    core_ref = core.astype(jnp.int32).reshape(1)
    share = embeddings.shape[0] // 2
    mine = lax.dynamic_slice_in_dim(embeddings, core * share, share, 0)
    blocks = len(row_groups[0])
    rows_a = to_group(jnp.broadcast_to(mine[None], (blocks,) + mine.shape), row_groups)
    rows_a = rows_a.reshape(blocks * share, -1)
    rows_b = lax.ppermute(rows_a, AXES, [(d, d ^ 1) for d in range(DEVICES)])
    cents, bias, highs, scores_a, scores_b = first_scores(centroids, rows_a)
    probs, own, message = second_scores(cents, rows_b, bias, highs, scores_a, scores_b)
    onward = merged(core_ref, to_group(message, plane_groups))
    received = to_group(onward, column_groups)
    return summed(core_ref, received, own, probs, rows_a, rows_b)


def solution(mesh):
    in_specs = (P("blk", None), P(AXES, None))
    out_specs = (P(AXES, None), P(AXES))
    return jax.shard_map(
        per_device, mesh=mesh, in_specs=in_specs, out_specs=out_specs, check_vma=False
    )
```

time: 801 us -> 67.7 us (0.08)
  the two profiles are of different devices: /device:TPU:32 before, /device:TPU:1 now
where the time goes in v2:
time: 67.7 us; the launch traced here: 67.5 us
  blocking collectives  48.8 us (72%)
  Pallas kernels  14.3 us (21%)
  starting transfers between devices  2.51 us (4%)
  local copies, waits for them, and re-layouts  1.06 us (2%)
  between operations  0.85 us (1%)
    all_to_all x3, blocking collectives, to_group(): lax.all_to_all(message, AXES, 0, 0, tiled=True, axis_index_groups=groups)  48.8 us
    pallas_call x4, Pallas kernels, call(): pl.pallas_call(kernel, out_shape=outs, in_specs=in_specs, out_specs=out_s...  14.3 us
    ppermute x1, starting transfers between devices, per_device(): rows_b = lax.ppermute(rows_a, AXES, [(d, d ^ 1) for d in range(DEVICES)])  2.51 us
  transfers between devices with their start and end apart: 1, of which 0 were waited for; matrix products, arithmetic and copies ran while one was open for 0% of the time, Pallas kernels for 7%

profile of v2, /device:TPU:1, one launch (start us, length us, event | category | flops | bytes accessed | tf_op | source)
XLA Modules:
  0.0 67.5 jit_solution(328747197586705065)
XLA Ops:
  0.6 0.0 copy-start
  0.7 0.9 %copy-done = bf16[128,1024]{1,0:T(8,128)(2,1)S(1)} copy-done((bf16[128,1024]{1,0:T(8,128)(2,1)S(1)}, bf16[128,1024]{1,0:T(8,128)(2,1)}, u32[]{:S(2)}) %copy-start) | copy-done | bytes 262168
  1.6 0.1 broadcast_in_dim.2
  1.7 22.3 %all_to_all.15 = bf16[8,64,1024]{2,1,0:T(8,128)(2,1)S(1)} all-to-all(bf16[8,64,1024]{2,1,0:T(8,128)(2,1)S(1)} %broadcast_in_dim.2), channel_id=1, replica_groups={{0,32,64,96,144,176,208,240},{1,33,65,97,145,177,209,241},{2,34,66,98,1..., dimensions={0} | all-to-all | bytes 2097152 | tf_op jit(solution)/shard_map/all_to_all | solution.py:275
  24.0 2.5 %collective-permute-start = (bf16[512,1024]{1,0:T(8,128)(2,1)S(1)}, bf16[512,1024]{1,0:T(8,128)(2,1)S(1)}, u32[]{:S(2)}, u32[]{:S(2)}) collective-permute-start(bf16[512,1024]{1,0:T(8,128)(2,1)S(1)} %bitcast.3), channel_id=1, source_target_pairs={{0,1},{1,0},{2,3},{3,2},{4,5},{5,4},{6,7},{7,6},{8,9},{9,8},{10,11... | collective-permute-start | bytes 3145736 | tf_op jit(solution)/shard_map/ppermute | solution.py:286
  26.5 4.5 %shard_map.41 = (bf16[2048,1024]{1,0:T(8,128)(2,1)S(1)}, f32[2048,128]{1,0:T(8,128)S(1)}, f32[2,256]{1,0:T(2,128)S(1)}, f32[2048,256]{1,0:T(8,128)S(1)}, f32[2048,256]{1,0:T(8,128)S(1)}) custom-call(bf16[2048,1024]{1,0:T(8,128)(2,1)} %source.1, bf16[512,1024]{1,0:T(8,128)(2,1)S(1)} %bitcast.4), custom_call_target="tpu_custom_call" | custom-call | tf_op jit(solution)/shard_map/pallas_call | solution.py:207
  31.1 0.0 collective-permute-done.rows.rows_b
  31.1 3.6 %shard_map.42 = (bf16[2048,1024]{1,0:T(8,128)(2,1)S(1)}, f32[8,128]{1,0:T(8,128)S(1)}, f32[16,8,128]{2,1,0:T(8,128)S(1)}) custom-call(bf16[2048,1024]{1,0:T(8,128)(2,1)S(1)} %get-tuple-element.12.cents, bf16[512,1024]{1,0:T(8,128)(2,1)S(1)} %collective-permute-done.rows.rows_b, f32[2048,128]{1,0:T(8,128)S(1)} %get-tuple-element.13.bias, ...), custom_call_target="tpu_custom_call" | custom-call | tf_op jit(solution)/shard_map/pallas_call | solution.py:207
  34.7 9.1 %all_to_all.16.received = f32[16,8,128]{2,1,0:T(8,128)S(1)} all-to-all(f32[16,8,128]{2,1,0:T(8,128)S(1)} %get-tuple-element.17), channel_id=1, replica_groups={{0,16,32,48,64,80,96,112,128,144,160,176,192,208,224,240},{1,17,33,49,6..., dimensions={0} | all-to-all | bytes 131072 | tf_op jit(solution)/shard_map/all_to_all | solution.py:275
  43.7 0.1 shard_map.43
  43.8 17.4 %all_to_all.17.received = f32[16,8,128]{2,1,0:T(8,128)S(1)} all-to-all(f32[16,8,128]{2,1,0:T(8,128)S(1)} %shard_map.43), channel_id=1, replica_groups={{0,1,2,3,4,5,6,7,8,9,10,11,12,13,14,15},{16,17,18,19,20,21,22,23,24,25,..., dimensions={0} | all-to-all | bytes 131072 | tf_op jit(solution)/shard_map/all_to_all | solution.py:275
  61.2 6.2 %shard_map.44 = (f32[2048,1024]{1,0:T(8,128)}, f32[16,128]{1,0:T(8,128)}) custom-call(s32[1]{0:T(128)} %bitcast.core, f32[16,8,128]{2,1,0:T(8,128)S(1)} %all_to_all.17.received, f32[8,128]{1,0:T(8,128)S(1)} %get-tuple-element.18.own, bf16[2048,1024]{1,0:T(8,128)(2,1)S(1)} %get-tuple-element.19.probs, bf16[512,1024]{1,0:T(8,128)(2,1)S(1)} %bitcast.5, ...), custom_call_target="tpu_custom_call" | custom-call | tf_op jit(solution)/shard_map/pallas_call | solution.py:207
  (1 shorter events, 0.0 us)
Async XLA Ops:
  0.6 1.0 %copy-start = (bf16[128,1024]{1,0:T(8,128)(2,1)S(1)}, bf16[128,1024]{1,0:T(8,128)(2,1)}, u32[]{:S(2)}) copy-start(bf16[128,1024]{1,0:T(8,128)(2,1)} %param.2) | copy-start | bytes 786436
  24.0 7.1 %collective-permute-start = (bf16[512,1024]{1,0:T(8,128)(2,1)S(1)}, bf16[512,1024]{1,0:T(8,128)(2,1)S(1)}, u32[]{:S(2)}, u32[]{:S(2)}) collective-permute-start(bf16[512,1024]{1,0:T(8,128)(2,1)S(1)} %bitcast.3), channel_id=1, source_target_pairs={{0,1},{1,0},{2,3},{3,2},{4,5},{5,4},{6,7},{7,6},{8,9},{9,8},{10,11... | collective-permute-start | bytes 3145736 | tf_op jit(solution)/shard_map/ppermute | solution.py:286

commit v3 on v2

v3 whole, which is shorter than its diff:
```python
import functools

import jax
import jax.numpy as jnp
from jax import lax
from jax.experimental import pallas as pl
from jax.experimental.pallas import tpu as pltpu
from jax.sharding import PartitionSpec as P

sharpness = 3.0
LOG2E = 1.4426950408889634
SCALE = sharpness * LOG2E
AXES = ("blk", "grp")
LANES = 128
ROW_TILE = 256
CENT_TILE = 256
OUT_COLS = 512
OUT_ROWS = 256
MIB = 1024 * 1024
ARRIVALS = ((0, 256), (256, 256), (512, 512), (1024, 512), (1536, 512))

DEVICES = 256
X_HI, Y, X_LO = 128, 32, 16


def groups_by(key):
    groups = {}
    for device in range(DEVICES):
        groups.setdefault(key(device), []).append(device)
    return list(groups.values())


def y_step(steps):
    return [(d, d // X_HI * X_HI + (d + steps * Y) % X_HI) for d in range(DEVICES)]


x_step = [(d, d ^ X_HI ^ X_LO) for d in range(DEVICES)]
core_step = [(d, d ^ 1) for d in range(DEVICES)]
Y_STEPS = (2, 1, 3)
plane_groups = groups_by(lambda d: d % X_LO)
column_groups = groups_by(lambda d: d // X_LO)


def in_vmem(value):
    return pltpu.with_memory_space_constraint(value, pltpu.VMEM)


def vmem_spec():
    return pl.BlockSpec(memory_space=pltpu.VMEM)


def part(i, size):
    return slice(i * size, (i + 1) * size)


def products(cents, rows, i):
    return lax.dot_general(
        cents[part(i, CENT_TILE), :],
        rows[...],
        (((1,), (1,)), ((), ())),
        preferred_element_type=jnp.float32,
    )


def shifted(block, bias):
    return block * SCALE + jnp.concatenate([bias] * (ROW_TILE // LANES), axis=1)


def fold(combine, block):
    return combine(block.reshape(-1, 8, block.shape[-1]), axis=0)


def no_highest():
    return jnp.full((8, ROW_TILE), -jnp.inf, jnp.float32)


def no_total():
    return jnp.zeros((8, ROW_TILE), jnp.float32)


def top(highest):
    return jnp.max(highest, axis=0, keepdims=True)


def whole(total):
    return jnp.sum(total, axis=0, keepdims=True)


def stacked(parts):
    return jnp.concatenate(
        [p[:, part(k, LANES)] for p in parts for k in range(p.shape[1] // LANES)], axis=0
    )


def exponentials(scores, highest, probs, i, column):
    block = jnp.exp2(scores[part(i, CENT_TILE), :] - highest)
    probs[part(i, CENT_TILE), part(column, ROW_TILE)] = block.astype(jnp.bfloat16)
    return fold(jnp.sum, block)


def arrange_kernel(device, *refs):
    blocks, rows = refs[:1 + len(Y_STEPS)], refs[-1]
    size = blocks[0].shape[0]
    y = device[0] // Y % 4
    for steps, block in zip((0,) + Y_STEPS, blocks):
        at = pl.multiple_of((y + 4 - steps) % 4 * size, size)
        rows[pl.ds(at, size), :] = block[...]


def first_kernel(source, rows, cents, bias, high, scores, arrived):
    copies = []
    for k, (start, size) in enumerate(ARRIVALS):
        at = pl.ds(start, size)
        copy = pltpu.make_async_copy(source.at[at, :], cents.at[at, :], arrived.at[k])
        copy.start()
        copies.append(copy)
    highest = no_highest()
    for copy, (start, size) in zip(copies, ARRIVALS):
        copy.wait()
        for i in range(start // CENT_TILE, (start + size) // CENT_TILE):
            block = cents[part(i, CENT_TILE), :].astype(jnp.float32)
            squared = jnp.sum(block * block, axis=1, keepdims=True)
            shift = jnp.broadcast_to(squared * (-0.5 * SCALE), (CENT_TILE, LANES))
            bias[part(i, CENT_TILE), :] = shift
            block = shifted(products(cents, rows, i), shift)
            scores[part(i, CENT_TILE), :] = block
            highest = jnp.maximum(highest, fold(jnp.max, block))
    high[...] = top(highest)


def score_step(cents, rows, bias, scores, before, highest_before, probs, column):
    highest, total = no_highest(), no_total()
    for i in range(cents.shape[0] // CENT_TILE):
        block = shifted(products(cents, rows, i), bias[part(i, CENT_TILE), :])
        scores[part(i, CENT_TILE), :] = block
        highest = jnp.maximum(highest, fold(jnp.max, block))
        total = total + exponentials(before, highest_before, probs, i, column)
    return top(highest), whole(total)


def middle_kernel(
    cents, bias, rows_b, rows_c, scores_a, high, probs, stats, scores_c, scores_b
):
    highest_a = high[...]
    highest_b, total_a = score_step(cents, rows_b, bias, scores_b, scores_a, highest_a, probs, 0)
    highest_c, total_b = score_step(cents, rows_c, bias, scores_c, scores_b, highest_b, probs, 1)
    stats[...] = jnp.concatenate([highest_a, highest_b, highest_c, total_a, total_b], axis=0)


def last_kernel(
    device, cents, bias, rows_d, scores_c, stats, probs, own, message, scores_d
):
    highest_c = stats[2:3, :]
    highest_d, total_c = score_step(cents, rows_d, bias, scores_d, scores_c, highest_c, probs, 0)
    total_d = no_total()
    for i in range(cents.shape[0] // CENT_TILE):
        total_d = total_d + exponentials(scores_d, highest_d, probs, i, 1)
    highest = stacked([stats[0:1, :], stats[1:2, :], highest_c, highest_d])
    total = stacked([stats[3:4, :], stats[4:5, :], total_c, whole(total_d)])
    own[...] = highest
    sent = by_x(device[0], highest + jnp.log(total) * LOG2E)
    message[...] = jnp.broadcast_to(sent[None], message.shape)


def combined(received):
    parts = [received[k] for k in range(received.shape[0])]
    highest = functools.reduce(jnp.maximum, parts)
    total = functools.reduce(jnp.add, [jnp.exp2(p - highest) for p in parts])
    return highest, total


def by_x(device, rows):
    quarter = rows.shape[0] // 4
    q = [rows[part(k, quarter)] for k in range(4)]
    return jnp.where(device // X_HI == 1, jnp.concatenate([q[1], q[0], q[3], q[2]], axis=0), rows)


def by_core(device, rows):
    half = rows.shape[0] // 2
    return jnp.where(device % 2 == 1, jnp.concatenate([rows[half:], rows[:half]], axis=0), rows)


def merge_kernel(device, received, message):
    highest, total = combined(received)
    merged = by_core(device[0], highest + jnp.log(total) * LOG2E)
    message[...] = jnp.broadcast_to(merged[None], message.shape)


def sum_kernel(
    device, received, own, probs_ab, probs_cd, rows_a, rows_b, rows_c, rows_d,
    sums, mass, scaled, out, masses, sent, mass_sent,
):
    cent_count, width = out.shape
    row_blocks = (rows_a, rows_b, rows_c, rows_d)
    block_tiles = ROW_TILE // LANES
    highest, total = (by_x(device[0], by_core(device[0], v)) for v in combined(received))
    factors = jnp.exp2(own[...] - highest) / total
    pieces = [(j, i) for j in range(width // OUT_COLS) for i in range(cent_count // OUT_ROWS)]
    tiles = cent_count // LANES
    copies = []
    for step, (j, i) in enumerate(pieces):
        columns = part(j, OUT_COLS)
        if i == 0:
            for k in range(4 * block_tiles):
                rows = row_blocks[k // block_tiles]
                factor = jnp.broadcast_to(factors[k:k + 1, :], (LANES, LANES)).T
                block = rows[part(k % block_tiles, LANES), columns].astype(jnp.float32)
                block = block * jnp.concatenate([factor] * (OUT_COLS // LANES), axis=1)
                scaled[part(k, LANES), columns] = block.astype(jnp.bfloat16)
        at = part(i, OUT_ROWS)
        weights = jnp.concatenate([probs_ab[at, :], probs_cd[at, :]], axis=1)
        out[at, columns] = jnp.dot(
            weights, scaled[:, columns], preferred_element_type=jnp.float32
        )
        copy = pltpu.make_async_copy(out.at[at, columns], sums.at[at, columns], sent.at[step])
        copy.start()
        copies.append(copy)
        for k in range(tiles * step // (len(pieces) - 2), min(tiles, tiles * (step + 1) // (len(pieces) - 2))):
            at = part(k, LANES)
            lanes = 0.0
            for probs, first in ((probs_ab, 0), (probs_cd, 2 * block_tiles)):
                for c in range(2 * block_tiles):
                    block = probs[at, part(c, LANES)].astype(jnp.float32)
                    lanes = lanes + block * factors[first + c:first + c + 1, :]
            masses[k:k + 1, :] = jnp.sum(lanes.T, axis=0, keepdims=True)
        if step == len(pieces) - 2:
            copy = pltpu.make_async_copy(masses, mass, mass_sent.at[0])
            copy.start()
            copies.append(copy)
    for copy in copies:
        copy.wait()


def call(kernel, inputs, in_specs, outs, out_specs, scratch, limit):
    return pl.pallas_call(
        kernel,
        out_shape=outs,
        in_specs=in_specs,
        out_specs=out_specs,
        scratch_shapes=scratch,
        compiler_params=pltpu.CompilerParams(vmem_limit_bytes=limit),
    )(*inputs)


def smem_spec():
    return pl.BlockSpec(memory_space=pltpu.SMEM)


def vmem_call(kernel, device, inputs, outs, scratch, limit):
    inputs = [in_vmem(v) for v in inputs]
    in_specs = [vmem_spec()] * len(inputs)
    if device is not None:
        inputs, in_specs = [device] + inputs, [smem_spec()] + in_specs
    return call(kernel, inputs, in_specs, outs, [vmem_spec()] * len(outs), scratch, limit)


def arranged(device, blocks, after=()):
    size, width = blocks[0].shape
    outs = (pltpu.VMEM((len(blocks) * size, width), blocks[0].dtype),)
    return vmem_call(arrange_kernel, device, blocks + list(after), outs, [], 4 * MIB)[0]


def first_scores(centroids, rows):
    count, width = centroids.shape
    outs = (
        pltpu.VMEM((count, width), centroids.dtype),
        pltpu.VMEM((count, LANES), jnp.float32),
        pltpu.VMEM((1, ROW_TILE), jnp.float32),
        pltpu.VMEM((count, ROW_TILE), jnp.float32),
    )
    scratch = [pltpu.SemaphoreType.DMA((len(ARRIVALS),))]
    in_specs = [pl.BlockSpec(memory_space=pltpu.HBM), vmem_spec()]
    inputs = (pltpu.with_memory_space_constraint(centroids, pltpu.HBM), in_vmem(rows))
    return call(first_kernel, inputs, in_specs, outs, [vmem_spec()] * len(outs), scratch, 8 * MIB)


def middle_scores(cents, bias, rows_b, rows_c, scores_a, high):
    count = cents.shape[0]
    outs = (
        pltpu.VMEM((count, 2 * ROW_TILE), jnp.bfloat16),
        pltpu.VMEM((5, ROW_TILE), jnp.float32),
        pltpu.VMEM((count, ROW_TILE), jnp.float32),
    )
    scratch = [pltpu.VMEM((count, ROW_TILE), jnp.float32)]
    inputs = (cents, bias, rows_b, rows_c, scores_a, high)
    return vmem_call(middle_kernel, None, inputs, outs, scratch, 8 * MIB)


def last_scores(device, cents, bias, rows_d, scores_c, stats):
    count = cents.shape[0]
    row_tiles = 4 * ROW_TILE // LANES
    outs = (
        pltpu.VMEM((count, 2 * ROW_TILE), jnp.bfloat16),
        pltpu.VMEM((row_tiles, LANES), jnp.float32),
        pltpu.VMEM((len(plane_groups[0]), row_tiles, LANES), jnp.float32),
    )
    scratch = [pltpu.VMEM((count, ROW_TILE), jnp.float32)]
    inputs = (cents, bias, rows_d, scores_c, stats)
    return vmem_call(last_kernel, device, inputs, outs, scratch, 8 * MIB)


def merged(device, received):
    outs = (pltpu.VMEM((len(column_groups[0]),) + received.shape[1:], jnp.float32),)
    return vmem_call(merge_kernel, device, (received,), outs, [], 4 * MIB)[0]


def summed(device, received, own, probs_ab, probs_cd, row_blocks):
    count, width = probs_ab.shape[0], row_blocks[0].shape[1]
    inputs = [in_vmem(v) for v in (received, own, probs_ab, probs_cd) + tuple(row_blocks)]
    outs = (
        jax.ShapeDtypeStruct((count, width), jnp.float32),
        jax.ShapeDtypeStruct((count // LANES, LANES), jnp.float32),
    )
    scratch = [
        pltpu.VMEM((4 * ROW_TILE, width), jnp.bfloat16),
        pltpu.VMEM((count, width), jnp.float32),
        pltpu.VMEM((count // LANES, LANES), jnp.float32),
        pltpu.SemaphoreType.DMA(((count // OUT_ROWS) * (width // OUT_COLS),)),
        pltpu.SemaphoreType.DMA((1,)),
    ]
    in_specs = [smem_spec()] + [vmem_spec()] * len(inputs)
    sums, mass = call(
        sum_kernel, [device] + inputs, in_specs, outs, [pl.BlockSpec(memory_space=pl.ANY)] * 2, scratch, 16 * MIB
    )
    return sums, mass.reshape(-1)


def to_group(message, groups):
    return lax.all_to_all(message, AXES, 0, 0, tiled=True, axis_index_groups=groups)


def per_device(embeddings, centroids):
    core = lax.axis_index("grp") % 2
    device = lax.axis_index(AXES).astype(jnp.int32).reshape(1)
    share = embeddings.shape[0] // 2
    mine = lax.dynamic_slice_in_dim(embeddings, core * share, share, 0)
    other = lax.ppermute(mine, AXES, x_step)
    near = [lax.ppermute(mine, AXES, y_step(steps)) for steps in Y_STEPS]
    far = [lax.ppermute(other, AXES, y_step(steps)) for steps in Y_STEPS]
    rows_a = arranged(device, [mine] + near)
    rows_c = lax.ppermute(rows_a, AXES, core_step)
    cents, bias, high, scores_a = first_scores(centroids, rows_a)
    rows_b = arranged(device, [other] + far, [high])
    rows_d = lax.ppermute(rows_b, AXES, core_step)
    probs_ab, stats, scores_c = middle_scores(cents, bias, rows_b, rows_c, scores_a, high)
    probs_cd, own, message = last_scores(device, cents, bias, rows_d, scores_c, stats)
    onward = merged(device, to_group(message, plane_groups))
    received = to_group(onward, column_groups)
    return summed(device, received, own, probs_ab, probs_cd, (rows_a, rows_b, rows_c, rows_d))


def solution(mesh):
    in_specs = (P("blk", None), P(AXES, None))
    out_specs = (P(AXES, None), P(AXES))
    return jax.shard_map(
        per_device, mesh=mesh, in_specs=in_specs, out_specs=out_specs, check_vma=False
    )
```

time: 67.7 us -> 62.1 us (0.917)
  blocking collectives: 48.8 us -> 26.8 us
  starting transfers between devices: 2.51 us -> 16.1 us
  waiting for transfers between devices: 0.01 us -> 2.17 us
  Pallas kernels: 14.3 us -> 15 us
    all_to_all x3 -> x2, blocking collectives: 48.8 us -> 26.8 us  [to_group(): lax.all_to_all(message, AXES, 0, 0, tiled=True, axis_index_groups=groups)]
    ppermute x1 -> x9, starting transfers between devices: 2.51 us -> 16.1 us  [the longest x1 4.63 us: per_device(): rows_c = lax.ppermute(rows_a, AXES, core_step)]
    ppermute x1 -> x9, waiting for transfers between devices: 0.01 us -> 2.17 us  [the longest x3 2.16 us: per_device(): near = [lax.ppermute(mine, AXES, y_step(steps)) for steps in Y_STEPS]]
    pallas_call x4 -> x7, Pallas kernels: 14.3 us -> 15 us  [call(): pl.pallas_call(kernel, out_shape=outs, in_specs=in_specs, out_specs=out_s...]
  transfers between devices with their start and end apart: 1 -> 9, of which waited for: 0 -> 1; matrix products, arithmetic and copies ran while one was open for 0% -> 0% of each run, Pallas kernels for 7% -> 11%
where the time goes in v3:
time: 62.1 us; the launch traced here: 61.9 us
  blocking collectives  26.8 us (43%)
  starting transfers between devices  16.1 us (26%)
  Pallas kernels  15 us (24%)
  waiting for transfers between devices  2.17 us (3%)
  local copies, waits for them, and re-layouts  0.94 us (2%)
  between operations  0.89 us (1%)
    all_to_all x2, blocking collectives, to_group(): lax.all_to_all(message, AXES, 0, 0, tiled=True, axis_index_groups=groups)  26.8 us
    pallas_call x7, Pallas kernels, call(): pl.pallas_call(kernel, out_shape=outs, in_specs=in_specs, out_specs=out_s...  15 us
    ppermute x1, starting transfers between devices, per_device(): rows_c = lax.ppermute(rows_a, AXES, core_step)  4.63 us
    ppermute x3, starting transfers between devices, per_device(): near = [lax.ppermute(mine, AXES, y_step(steps)) for steps in Y_STEPS]  4.38 us
    ppermute x3, starting transfers between devices, per_device(): far = [lax.ppermute(other, AXES, y_step(steps)) for steps in Y_STEPS]  3.4 us
    ppermute x1, starting transfers between devices, per_device(): other = lax.ppermute(mine, AXES, x_step)  3.39 us
    ppermute x3, waiting for transfers between devices, per_device(): near = [lax.ppermute(mine, AXES, y_step(steps)) for steps in Y_STEPS]  2.16 us
  transfers between devices with their start and end apart: 9, of which 1 were waited for; matrix products, arithmetic and copies ran while one was open for 0% of the time, Pallas kernels for 11%

profile of v3, /device:TPU:1, one launch (start us, length us, event | category | flops | bytes accessed | tf_op | source)
XLA Modules:
  0.0 61.9 jit_solution(8290037211811541008)
XLA Ops:
  0.6 0.0 copy-start
  0.7 0.9 %copy-done = bf16[128,1024]{1,0:T(8,128)(2,1)S(1)} copy-done((bf16[128,1024]{1,0:T(8,128)(2,1)S(1)}, bf16[128,1024]{1,0:T(8,128)(2,1)}, u32[]{:S(2)}) %copy-start) | copy-done | bytes 262168
  1.6 3.4 %collective-permute-start.3 = (bf16[64,1024]{1,0:T(8,128)(2,1)S(1)}, bf16[64,1024]{1,0:T(8,128)(2,1)S(1)}, u32[]{:S(2)}, u32[]{:S(2)}) collective-permute-start(bf16[64,1024]{1,0:T(8,128)(2,1)S(1)} %constant_dynamic-slice_fusion.refs_0_), channel_id=1, source_target_pairs={{0,144},{1,145},{2,146},{3,147},{4,148},{5,149},{6,150},{7,151},{8... | collective-permute-start | bytes 393224 | tf_op jit(solution)/shard_map/ppermute | solution.py:337
  5.0 2.7 %collective-permute-start.2 = (bf16[64,1024]{1,0:T(8,128)(2,1)S(1)}, bf16[64,1024]{1,0:T(8,128)(2,1)S(1)}, u32[]{:S(2)}, u32[]{:S(2)}) collective-permute-start(bf16[64,1024]{1,0:T(8,128)(2,1)S(1)} %constant_dynamic-slice_fusion.refs_0_), channel_id=1, source_target_pairs={{0,96},{1,97},{2,98},{3,99},{4,100},{5,101},{6,102},{7,103},{8,104... | collective-permute-start | bytes 393224 | tf_op jit(solution)/shard_map/ppermute | solution.py:338
  7.7 0.0 collective-permute-start.1
  7.7 1.6 %collective-permute-start = (bf16[64,1024]{1,0:T(8,128)(2,1)S(1)}, bf16[64,1024]{1,0:T(8,128)(2,1)S(1)}, u32[]{:S(2)}, u32[]{:S(2)}) collective-permute-start(bf16[64,1024]{1,0:T(8,128)(2,1)S(1)} %constant_dynamic-slice_fusion.refs_0_), channel_id=1, source_target_pairs={{0,64},{1,65},{2,66},{3,67},{4,68},{5,69},{6,70},{7,71},{8,72},{9,... | collective-permute-start | bytes 393224 | tf_op jit(solution)/shard_map/ppermute | solution.py:338
  9.4 0.0 collective-permute-done.3.refs_0_
  9.4 1.4 %collective-permute-start.6 = (bf16[64,1024]{1,0:T(8,128)(2,1)S(1)}, bf16[64,1024]{1,0:T(8,128)(2,1)S(1)}, u32[]{:S(2)}, u32[]{:S(2)}) collective-permute-start(bf16[64,1024]{1,0:T(8,128)(2,1)S(1)} %collective-permute-done.3.refs_0_), channel_id=1, source_target_pairs={{0,96},{1,97},{2,98},{3,99},{4,100},{5,101},{6,102},{7,103},{8,104... | collective-permute-start | bytes 393224 | tf_op jit(solution)/shard_map/ppermute | solution.py:339
  10.8 0.2 collective-permute-start.5
  11.0 0.0 collective-permute-done.2.refs_3_
  11.0 1.8 %collective-permute-start.4 = (bf16[64,1024]{1,0:T(8,128)(2,1)S(1)}, bf16[64,1024]{1,0:T(8,128)(2,1)S(1)}, u32[]{:S(2)}, u32[]{:S(2)}) collective-permute-start(bf16[64,1024]{1,0:T(8,128)(2,1)S(1)} %collective-permute-done.3.refs_0_), channel_id=1, source_target_pairs={{0,64},{1,65},{2,66},{3,67},{4,68},{5,69},{6,70},{7,71},{8,72},{9,... | collective-permute-start | bytes 393224 | tf_op jit(solution)/shard_map/ppermute | solution.py:339
  12.8 2.2 %collective-permute-done.1.refs_2_ = bf16[64,1024]{1,0:T(8,128)(2,1)S(1)} collective-permute-done((bf16[64,1024]{1,0:T(8,128)(2,1)S(1)}, bf16[64,1024]{1,0:T(8,128)(2,1)S(1)}, u32[]{:S(2)}, u32[]{:S(2)}) %collective-permute-start.1) | collective-permute-done | bytes 131104 | tf_op jit(solution)/shard_map/ppermute | solution.py:338
  14.9 0.0 collective-permute-done.refs_1_
  15.0 4.6 %collective-permute-start.8 = (bf16[256,1024]{1,0:T(8,128)(2,1)S(1)}, bf16[256,1024]{1,0:T(8,128)(2,1)S(1)}, u32[]{:S(2)}, u32[]{:S(2)}) collective-permute-start(bf16[256,1024]{1,0:T(8,128)(2,1)S(1)} %shard_map.41.rows.rows_a), channel_id=1, source_target_pairs={{0,1},{1,0},{2,3},{3,2},{4,5},{5,4},{6,7},{7,6},{8,9},{9,8},{10,11... | collective-permute-start | bytes 1572872 | tf_op jit(solution)/shard_map/ppermute | solution.py:341
  19.6 3.6 %shard_map.42 = (bf16[2048,1024]{1,0:T(8,128)(2,1)S(1)}, f32[2048,128]{1,0:T(8,128)S(1)}, f32[1,256]{1,0:T(1,128)S(1)}, f32[2048,256]{1,0:T(8,128)S(1)}) custom-call(bf16[2048,1024]{1,0:T(8,128)(2,1)} %source.1, bf16[256,1024]{1,0:T(8,128)(2,1)S(1)} %shard_map.41.rows.rows_a), custom_call_target="tpu_custom_call" | custom-call | tf_op jit(solution)/shard_map/pallas_call | solution.py:235
  23.3 0.0 collective-permute-done.6.refs_3_
  23.3 0.0 collective-permute-done.5.refs_2_
  23.3 0.0 collective-permute-done.4.refs_1_
  23.3 0.1 shard_map.43.rows_b
  23.4 0.3 collective-permute-start.7
  23.7 0.0 collective-permute-done.8.rows_c
  23.7 3.1 %shard_map.44 = (bf16[2048,512]{1,0:T(8,128)(2,1)S(1)}, f32[5,256]{1,0:T(8,128)S(1)}, f32[2048,256]{1,0:T(8,128)S(1)}) custom-call(bf16[2048,1024]{1,0:T(8,128)(2,1)S(1)} %get-tuple-element.14.cents, f32[2048,128]{1,0:T(8,128)S(1)} %get-tuple-element.15.bias, bf16[256,1024]{1,0:T(8,128)(2,1)S(1)} %shard_map.43.rows_b, ...), custom_call_target="tpu_custom_call" | custom-call | tf_op jit(solution)/shard_map/pallas_call | solution.py:235
  26.8 0.0 collective-permute-done.7.rows_d
  26.8 2.0 %shard_map.45 = (bf16[2048,512]{1,0:T(8,128)(2,1)S(1)}, f32[8,128]{1,0:T(8,128)S(1)}, f32[16,8,128]{2,1,0:T(8,128)S(1)}) custom-call(s32[1]{0:T(128)} %bitcast.device, bf16[2048,1024]{1,0:T(8,128)(2,1)S(1)} %get-tuple-element.14.cents, f32[2048,128]{1,0:T(8,128)S(1)} %get-tuple-element.15.bias, bf16[256,1024]{1,0:T(8,128)(2,1)S(1)} %collective-permute-done.7.rows_d, ...), custom_call_target="tpu_custom_call" | custom-call | tf_op jit(solution)/shard_map/pallas_call | solution.py:235
  28.8 9.1 %all_to_all.10.received = f32[16,8,128]{2,1,0:T(8,128)S(1)} all-to-all(f32[16,8,128]{2,1,0:T(8,128)S(1)} %get-tuple-element.20), channel_id=1, replica_groups={{0,16,32,48,64,80,96,112,128,144,160,176,192,208,224,240},{1,17,33,49,6..., dimensions={0} | all-to-all | bytes 131072 | tf_op jit(solution)/shard_map/all_to_all | solution.py:329
  37.8 0.1 shard_map.46
  37.9 17.7 %all_to_all.11.received = f32[16,8,128]{2,1,0:T(8,128)S(1)} all-to-all(f32[16,8,128]{2,1,0:T(8,128)S(1)} %shard_map.46), channel_id=1, replica_groups={{0,1,2,3,4,5,6,7,8,9,10,11,12,13,14,15},{16,17,18,19,20,21,22,23,24,25,..., dimensions={0} | all-to-all | bytes 131072 | tf_op jit(solution)/shard_map/all_to_all | solution.py:329
  55.6 6.2 %shard_map.47 = (f32[2048,1024]{1,0:T(8,128)}, f32[16,128]{1,0:T(8,128)}) custom-call(s32[1]{0:T(128)} %bitcast.device, f32[16,8,128]{2,1,0:T(8,128)S(1)} %all_to_all.11.received, f32[8,128]{1,0:T(8,128)S(1)} %get-tuple-element.21.own, bf16[2048,512]{1,0:T(8,128)(2,1)S(1)} %get-tuple-element.22.probs_ab, bf16[2048,512]{1,0:T(8,128)(2,1)S(1)} %get-tuple-element.23.probs_cd, ...), custom_call_target="tpu_custom_call" | custom-call | tf_op jit(solution)/shard_map/pallas_call | solution.py:235
  (2 shorter events, 0.1 us)
Async XLA Ops:
  0.6 1.0 %copy-start = (bf16[128,1024]{1,0:T(8,128)(2,1)S(1)}, bf16[128,1024]{1,0:T(8,128)(2,1)}, u32[]{:S(2)}) copy-start(bf16[128,1024]{1,0:T(8,128)(2,1)} %param.2) | copy-start | bytes 786436
  1.6 7.8 %collective-permute-start.3 = (bf16[64,1024]{1,0:T(8,128)(2,1)S(1)}, bf16[64,1024]{1,0:T(8,128)(2,1)S(1)}, u32[]{:S(2)}, u32[]{:S(2)}) collective-permute-start(bf16[64,1024]{1,0:T(8,128)(2,1)S(1)} %constant_dynamic-slice_fusion.refs_0_), channel_id=1, source_target_pairs={{0,144},{1,145},{2,146},{3,147},{4,148},{5,149},{6,150},{7,151},{8... | collective-permute-start | bytes 393224 | tf_op jit(solution)/shard_map/ppermute | solution.py:337
  5.0 6.0 %collective-permute-start.2 = (bf16[64,1024]{1,0:T(8,128)(2,1)S(1)}, bf16[64,1024]{1,0:T(8,128)(2,1)S(1)}, u32[]{:S(2)}, u32[]{:S(2)}) collective-permute-start(bf16[64,1024]{1,0:T(8,128)(2,1)S(1)} %constant_dynamic-slice_fusion.refs_0_), channel_id=1, source_target_pairs={{0,96},{1,97},{2,98},{3,99},{4,100},{5,101},{6,102},{7,103},{8,104... | collective-permute-start | bytes 393224 | tf_op jit(solution)/shard_map/ppermute | solution.py:338
  7.7 7.2 %collective-permute-start.1 = (bf16[64,1024]{1,0:T(8,128)(2,1)S(1)}, bf16[64,1024]{1,0:T(8,128)(2,1)S(1)}, u32[]{:S(2)}, u32[]{:S(2)}) collective-permute-start(bf16[64,1024]{1,0:T(8,128)(2,1)S(1)} %constant_dynamic-slice_fusion.refs_0_), channel_id=1, source_target_pairs={{0,32},{1,33},{2,34},{3,35},{4,36},{5,37},{6,38},{7,39},{8,40},{9,... | collective-permute-start | bytes 393224 | tf_op jit(solution)/shard_map/ppermute | solution.py:338
  7.7 7.2 %collective-permute-start = (bf16[64,1024]{1,0:T(8,128)(2,1)S(1)}, bf16[64,1024]{1,0:T(8,128)(2,1)S(1)}, u32[]{:S(2)}, u32[]{:S(2)}) collective-permute-start(bf16[64,1024]{1,0:T(8,128)(2,1)S(1)} %constant_dynamic-slice_fusion.refs_0_), channel_id=1, source_target_pairs={{0,64},{1,65},{2,66},{3,67},{4,68},{5,69},{6,70},{7,71},{8,72},{9,... | collective-permute-start | bytes 393224 | tf_op jit(solution)/shard_map/ppermute | solution.py:338
  9.4 13.9 %collective-permute-start.6 = (bf16[64,1024]{1,0:T(8,128)(2,1)S(1)}, bf16[64,1024]{1,0:T(8,128)(2,1)S(1)}, u32[]{:S(2)}, u32[]{:S(2)}) collective-permute-start(bf16[64,1024]{1,0:T(8,128)(2,1)S(1)} %collective-permute-done.3.refs_0_), channel_id=1, source_target_pairs={{0,96},{1,97},{2,98},{3,99},{4,100},{5,101},{6,102},{7,103},{8,104... | collective-permute-start | bytes 393224 | tf_op jit(solution)/shard_map/ppermute | solution.py:339
  10.8 12.5 %collective-permute-start.5 = (bf16[64,1024]{1,0:T(8,128)(2,1)S(1)}, bf16[64,1024]{1,0:T(8,128)(2,1)S(1)}, u32[]{:S(2)}, u32[]{:S(2)}) collective-permute-start(bf16[64,1024]{1,0:T(8,128)(2,1)S(1)} %collective-permute-done.3.refs_0_), channel_id=1, source_target_pairs={{0,32},{1,33},{2,34},{3,35},{4,36},{5,37},{6,38},{7,39},{8,40},{9,... | collective-permute-start | bytes 393224 | tf_op jit(solution)/shard_map/ppermute | solution.py:339
  11.0 12.3 %collective-permute-start.4 = (bf16[64,1024]{1,0:T(8,128)(2,1)S(1)}, bf16[64,1024]{1,0:T(8,128)(2,1)S(1)}, u32[]{:S(2)}, u32[]{:S(2)}) collective-permute-start(bf16[64,1024]{1,0:T(8,128)(2,1)S(1)} %collective-permute-done.3.refs_0_), channel_id=1, source_target_pairs={{0,64},{1,65},{2,66},{3,67},{4,68},{5,69},{6,70},{7,71},{8,72},{9,... | collective-permute-start | bytes 393224 | tf_op jit(solution)/shard_map/ppermute | solution.py:339
  15.0 8.7 %collective-permute-start.8 = (bf16[256,1024]{1,0:T(8,128)(2,1)S(1)}, bf16[256,1024]{1,0:T(8,128)(2,1)S(1)}, u32[]{:S(2)}, u32[]{:S(2)}) collective-permute-start(bf16[256,1024]{1,0:T(8,128)(2,1)S(1)} %shard_map.41.rows.rows_a), channel_id=1, source_target_pairs={{0,1},{1,0},{2,3},{3,2},{4,5},{5,4},{6,7},{7,6},{8,9},{9,8},{10,11... | collective-permute-start | bytes 1572872 | tf_op jit(solution)/shard_map/ppermute | solution.py:341
  23.4 3.4 %collective-permute-start.7 = (bf16[256,1024]{1,0:T(8,128)(2,1)S(1)}, bf16[256,1024]{1,0:T(8,128)(2,1)S(1)}, u32[]{:S(2)}, u32[]{:S(2)}) collective-permute-start(bf16[256,1024]{1,0:T(8,128)(2,1)S(1)} %shard_map.43.rows_b), channel_id=1, source_target_pairs={{0,1},{1,0},{2,3},{3,2},{4,5},{5,4},{6,7},{7,6},{8,9},{9,8},{10,11... | collective-permute-start | bytes 1572872 | tf_op jit(solution)/shard_map/ppermute | solution.py:344

commit v4 on v3

--- a/solution.py
+++ b/solution.py
@@ -107,24 +107,30 @@
         rows[pl.ds(at, size), :] = block[...]
 
 
-def first_kernel(source, rows, cents, bias, high, scores, arrived):
+def bias_kernel(device, source, cents, bias, ready, arrived):
+    ready[...] = jnp.zeros_like(ready)
     copies = []
     for k, (start, size) in enumerate(ARRIVALS):
         at = pl.ds(start, size)
         copy = pltpu.make_async_copy(source.at[at, :], cents.at[at, :], arrived.at[k])
         copy.start()
         copies.append(copy)
-    highest = no_highest()
     for copy, (start, size) in zip(copies, ARRIVALS):
         copy.wait()
         for i in range(start // CENT_TILE, (start + size) // CENT_TILE):
             block = cents[part(i, CENT_TILE), :].astype(jnp.float32)
             squared = jnp.sum(block * block, axis=1, keepdims=True)
-            shift = jnp.broadcast_to(squared * (-0.5 * SCALE), (CENT_TILE, LANES))
-            bias[part(i, CENT_TILE), :] = shift
-            block = shifted(products(cents, rows, i), shift)
-            scores[part(i, CENT_TILE), :] = block
-            highest = jnp.maximum(highest, fold(jnp.max, block))
+            bias[part(i, CENT_TILE), :] = jnp.broadcast_to(
+                squared * (-0.5 * SCALE), (CENT_TILE, LANES)
+            )
+
+
+def first_kernel(cents, bias, rows, high, scores):
+    highest = no_highest()
+    for i in range(cents.shape[0] // CENT_TILE):
+        block = shifted(products(cents, rows, i), bias[part(i, CENT_TILE), :])
+        scores[part(i, CENT_TILE), :] = block
+        highest = jnp.maximum(highest, fold(jnp.max, block))
     high[...] = top(highest)
 
 
@@ -260,18 +266,23 @@
     return vmem_call(arrange_kernel, device, blocks + list(after), outs, [], 4 * MIB)[0]
 
 
-def first_scores(centroids, rows):
+def biased(device, centroids):
     count, width = centroids.shape
     outs = (
         pltpu.VMEM((count, width), centroids.dtype),
         pltpu.VMEM((count, LANES), jnp.float32),
-        pltpu.VMEM((1, ROW_TILE), jnp.float32),
-        pltpu.VMEM((count, ROW_TILE), jnp.float32),
+        pltpu.VMEM((8, LANES), jnp.float32),
     )
     scratch = [pltpu.SemaphoreType.DMA((len(ARRIVALS),))]
-    in_specs = [pl.BlockSpec(memory_space=pltpu.HBM), vmem_spec()]
-    inputs = (pltpu.with_memory_space_constraint(centroids, pltpu.HBM), in_vmem(rows))
-    return call(first_kernel, inputs, in_specs, outs, [vmem_spec()] * len(outs), scratch, 8 * MIB)
+    in_specs = [smem_spec(), pl.BlockSpec(memory_space=pltpu.HBM)]
+    inputs = (device, pltpu.with_memory_space_constraint(centroids, pltpu.HBM))
+    return call(bias_kernel, inputs, in_specs, outs, [vmem_spec()] * len(outs), scratch, 4 * MIB)
+
+
+def first_scores(cents, bias, rows):
+    count = cents.shape[0]
+    outs = (pltpu.VMEM((1, ROW_TILE), jnp.float32), pltpu.VMEM((count, ROW_TILE), jnp.float32))
+    return vmem_call(first_kernel, None, (cents, bias, rows), outs, [], 4 * MIB)
 
 
 def middle_scores(cents, bias, rows_b, rows_c, scores_a, high):
@@ -335,12 +346,13 @@
     share = embeddings.shape[0] // 2
     mine = lax.dynamic_slice_in_dim(embeddings, core * share, share, 0)
     other = lax.ppermute(mine, AXES, x_step)
+    cents, bias, ready = biased(device, centroids)
     near = [lax.ppermute(mine, AXES, y_step(steps)) for steps in Y_STEPS]
     far = [lax.ppermute(other, AXES, y_step(steps)) for steps in Y_STEPS]
-    rows_a = arranged(device, [mine] + near)
+    rows_a = arranged(device, [mine] + near, [ready])
     rows_c = lax.ppermute(rows_a, AXES, core_step)
-    cents, bias, high, scores_a = first_scores(centroids, rows_a)
-    rows_b = arranged(device, [other] + far, [high])
+    high, scores_a = first_scores(cents, bias, rows_a)
+    rows_b = arranged(device, [other] + far, [high, ready])
     rows_d = lax.ppermute(rows_b, AXES, core_step)
     probs_ab, stats, scores_c = middle_scores(cents, bias, rows_b, rows_c, scores_a, high)
     probs_cd, own, message = last_scores(device, cents, bias, rows_d, scores_c, stats)

time: 62.1 us -> 61.5 us (level)
  waiting for transfers between devices: 2.17 us -> 1.03 us
  starting transfers between devices: 16.1 us -> 17 us
    ppermute x3, waiting for transfers between devices: 2.16 us -> 0.01 us  [per_device(): near = [lax.ppermute(mine, AXES, y_step(steps)) for steps in Y_STEPS]]
    ppermute x1, starting transfers between devices: 0.29 us -> 1.59 us  [per_device(): rows_d = lax.ppermute(rows_b, AXES, core_step)]
    ppermute x3, waiting for transfers between devices: 0.01 us -> 1.01 us  [per_device(): far = [lax.ppermute(other, AXES, y_step(steps)) for steps in Y_STEPS]]
    pallas_call x7 -> x8, Pallas kernels: 15 us -> 15.2 us  [call(): pl.pallas_call(kernel, out_shape=outs, in_specs=in_specs, out_specs=out_s...]
where the time goes in v4:
time: 61.5 us; the launch traced here: 61.4 us
  blocking collectives  26.3 us (43%)
  starting transfers between devices  17 us (28%)
  Pallas kernels  15.2 us (25%)
  waiting for transfers between devices  1.03 us (2%)
  local copies, waits for them, and re-layouts  0.94 us (2%)
  between operations  0.89 us (1%)
    all_to_all x2, blocking collectives, to_group(): lax.all_to_all(message, AXES, 0, 0, tiled=True, axis_index_groups=groups)  26.3 us
    pallas_call x8, Pallas kernels, call(): pl.pallas_call(kernel, out_shape=outs, in_specs=in_specs, out_specs=out_s...  15.2 us
    ppermute x3, starting transfers between devices, per_device(): near = [lax.ppermute(mine, AXES, y_step(steps)) for steps in Y_STEPS]  4.38 us
    ppermute x1, starting transfers between devices, per_device(): rows_c = lax.ppermute(rows_a, AXES, core_step)  4.26 us
    ppermute x3, starting transfers between devices, per_device(): far = [lax.ppermute(other, AXES, y_step(steps)) for steps in Y_STEPS]  3.4 us
    ppermute x1, starting transfers between devices, per_device(): other = lax.ppermute(mine, AXES, x_step)  3.39 us
    ppermute x1, starting transfers between devices, per_device(): rows_d = lax.ppermute(rows_b, AXES, core_step)  1.59 us
  transfers between devices with their start and end apart: 9, of which 1 were waited for; matrix products, arithmetic and copies ran while one was open for 0% of the time, Pallas kernels for 11%

profile of v4, /device:TPU:1, one launch (start us, length us, event | category | flops | bytes accessed | tf_op | source)
XLA Modules:
  0.0 61.4 jit_solution(2567170084503238432)
XLA Ops:
  0.6 0.0 copy-start
  0.7 0.9 %copy-done = bf16[128,1024]{1,0:T(8,128)(2,1)S(1)} copy-done((bf16[128,1024]{1,0:T(8,128)(2,1)S(1)}, bf16[128,1024]{1,0:T(8,128)(2,1)}, u32[]{:S(2)}) %copy-start) | copy-done | bytes 262168
  1.6 3.4 %collective-permute-start = (bf16[64,1024]{1,0:T(8,128)(2,1)S(1)}, bf16[64,1024]{1,0:T(8,128)(2,1)S(1)}, u32[]{:S(2)}, u32[]{:S(2)}) collective-permute-start(bf16[64,1024]{1,0:T(8,128)(2,1)S(1)} %constant_dynamic-slice_fusion.refs_0_), channel_id=1, source_target_pairs={{0,144},{1,145},{2,146},{3,147},{4,148},{5,149},{6,150},{7,151},{8... | collective-permute-start | bytes 393224 | tf_op jit(solution)/shard_map/ppermute | solution.py:348
  5.0 2.7 %collective-permute-start.6 = (bf16[64,1024]{1,0:T(8,128)(2,1)S(1)}, bf16[64,1024]{1,0:T(8,128)(2,1)S(1)}, u32[]{:S(2)}, u32[]{:S(2)}) collective-permute-start(bf16[64,1024]{1,0:T(8,128)(2,1)S(1)} %constant_dynamic-slice_fusion.refs_0_), channel_id=1, source_target_pairs={{0,96},{1,97},{2,98},{3,99},{4,100},{5,101},{6,102},{7,103},{8,104... | collective-permute-start | bytes 393224 | tf_op jit(solution)/shard_map/ppermute | solution.py:350
  7.7 0.0 collective-permute-start.5
  7.7 1.6 %collective-permute-start.4 = (bf16[64,1024]{1,0:T(8,128)(2,1)S(1)}, bf16[64,1024]{1,0:T(8,128)(2,1)S(1)}, u32[]{:S(2)}, u32[]{:S(2)}) collective-permute-start(bf16[64,1024]{1,0:T(8,128)(2,1)S(1)} %constant_dynamic-slice_fusion.refs_0_), channel_id=1, source_target_pairs={{0,64},{1,65},{2,66},{3,67},{4,68},{5,69},{6,70},{7,71},{8,72},{9,... | collective-permute-start | bytes 393224 | tf_op jit(solution)/shard_map/ppermute | solution.py:350
  9.4 0.0 collective-permute-done.refs_0_
  9.4 1.4 %collective-permute-start.3 = (bf16[64,1024]{1,0:T(8,128)(2,1)S(1)}, bf16[64,1024]{1,0:T(8,128)(2,1)S(1)}, u32[]{:S(2)}, u32[]{:S(2)}) collective-permute-start(bf16[64,1024]{1,0:T(8,128)(2,1)S(1)} %collective-permute-done.refs_0_), channel_id=1, source_target_pairs={{0,96},{1,97},{2,98},{3,99},{4,100},{5,101},{6,102},{7,103},{8,104... | collective-permute-start | bytes 393224 | tf_op jit(solution)/shard_map/ppermute | solution.py:351
  10.8 0.2 collective-permute-start.2
  11.0 0.0 collective-permute-done.6.refs_3_
  11.0 1.8 %collective-permute-start.1 = (bf16[64,1024]{1,0:T(8,128)(2,1)S(1)}, bf16[64,1024]{1,0:T(8,128)(2,1)S(1)}, u32[]{:S(2)}, u32[]{:S(2)}) collective-permute-start(bf16[64,1024]{1,0:T(8,128)(2,1)S(1)} %collective-permute-done.refs_0_), channel_id=1, source_target_pairs={{0,64},{1,65},{2,66},{3,67},{4,68},{5,69},{6,70},{7,71},{8,72},{9,... | collective-permute-start | bytes 393224 | tf_op jit(solution)/shard_map/ppermute | solution.py:351
  12.8 2.5 %shard_map.41 = (bf16[2048,1024]{1,0:T(8,128)(2,1)S(1)}, f32[2048,128]{1,0:T(8,128)S(1)}, f32[8,128]{1,0:T(8,128)S(1)}) custom-call(s32[1]{0:T(128)} %bitcast.device, bf16[2048,1024]{1,0:T(8,128)(2,1)} %source.1), custom_call_target="tpu_custom_call" | custom-call | tf_op jit(solution)/shard_map/pallas_call | solution.py:241
  15.3 0.0 collective-permute-done.5.refs_2_
  15.3 0.0 collective-permute-done.4.refs_1_
  15.3 0.1 shard_map.42.rows.rows_a
  15.4 4.3 %collective-permute-start.8 = (bf16[256,1024]{1,0:T(8,128)(2,1)S(1)}, bf16[256,1024]{1,0:T(8,128)(2,1)S(1)}, u32[]{:S(2)}, u32[]{:S(2)}) collective-permute-start(bf16[256,1024]{1,0:T(8,128)(2,1)S(1)} %shard_map.42.rows.rows_a), channel_id=1, source_target_pairs={{0,1},{1,0},{2,3},{3,2},{4,5},{5,4},{6,7},{7,6},{8,9},{9,8},{10,11... | collective-permute-start | bytes 1572872 | tf_op jit(solution)/shard_map/ppermute | solution.py:353
  19.6 1.3 %shard_map.43 = (f32[1,256]{1,0:T(1,128)S(1)}, f32[2048,256]{1,0:T(8,128)S(1)}) custom-call(bf16[2048,1024]{1,0:T(8,128)(2,1)S(1)} %get-tuple-element.15.cents, f32[2048,128]{1,0:T(8,128)S(1)} %get-tuple-element.16.bias, bf16[256,1024]{1,0:T(8,128)(2,1)S(1)} %shard_map.42.rows.rows_a), custom_call_target="tpu_custom_call" | custom-call | tf_op jit(solution)/shard_map/pallas_call | solution.py:241
  20.9 0.0 collective-permute-done.3.refs_3_
  21.0 1.0 %collective-permute-done.2.refs_2_ = bf16[64,1024]{1,0:T(8,128)(2,1)S(1)} collective-permute-done((bf16[64,1024]{1,0:T(8,128)(2,1)S(1)}, bf16[64,1024]{1,0:T(8,128)(2,1)S(1)}, u32[]{:S(2)}, u32[]{:S(2)}) %collective-permute-start.2) | collective-permute-done | bytes 131104 | tf_op jit(solution)/shard_map/ppermute | solution.py:351
  22.0 0.0 collective-permute-done.1.refs_1_
  22.0 1.6 %collective-permute-start.7 = (bf16[256,1024]{1,0:T(8,128)(2,1)S(1)}, bf16[256,1024]{1,0:T(8,128)(2,1)S(1)}, u32[]{:S(2)}, u32[]{:S(2)}) collective-permute-start(bf16[256,1024]{1,0:T(8,128)(2,1)S(1)} %shard_map.44.rows_b), channel_id=1, source_target_pairs={{0,1},{1,0},{2,3},{3,2},{4,5},{5,4},{6,7},{7,6},{8,9},{9,8},{10,11... | collective-permute-start | bytes 1572872 | tf_op jit(solution)/shard_map/ppermute | solution.py:356
  23.6 0.0 collective-permute-done.8.rows_c
  23.6 3.1 %shard_map.45 = (bf16[2048,512]{1,0:T(8,128)(2,1)S(1)}, f32[5,256]{1,0:T(8,128)S(1)}, f32[2048,256]{1,0:T(8,128)S(1)}) custom-call(bf16[2048,1024]{1,0:T(8,128)(2,1)S(1)} %get-tuple-element.15.cents, f32[2048,128]{1,0:T(8,128)S(1)} %get-tuple-element.16.bias, bf16[256,1024]{1,0:T(8,128)(2,1)S(1)} %shard_map.44.rows_b, ...), custom_call_target="tpu_custom_call" | custom-call | tf_op jit(solution)/shard_map/pallas_call | solution.py:241
  26.7 0.0 collective-permute-done.7.rows_d
  26.7 2.0 %shard_map.46 = (bf16[2048,512]{1,0:T(8,128)(2,1)S(1)}, f32[8,128]{1,0:T(8,128)S(1)}, f32[16,8,128]{2,1,0:T(8,128)S(1)}) custom-call(s32[1]{0:T(128)} %bitcast.device, bf16[2048,1024]{1,0:T(8,128)(2,1)S(1)} %get-tuple-element.15.cents, f32[2048,128]{1,0:T(8,128)S(1)} %get-tuple-element.16.bias, bf16[256,1024]{1,0:T(8,128)(2,1)S(1)} %collective-permute-done.7.rows_d, ...), custom_call_target="tpu_custom_call" | custom-call | tf_op jit(solution)/shard_map/pallas_call | solution.py:241
  28.7 9.4 %all_to_all.10.received = f32[16,8,128]{2,1,0:T(8,128)S(1)} all-to-all(f32[16,8,128]{2,1,0:T(8,128)S(1)} %get-tuple-element.22), channel_id=1, replica_groups={{0,16,32,48,64,80,96,112,128,144,160,176,192,208,224,240},{1,17,33,49,6..., dimensions={0} | all-to-all | bytes 131072 | tf_op jit(solution)/shard_map/all_to_all | solution.py:340
  38.0 0.1 shard_map.47
  38.1 17.0 %all_to_all.11.received = f32[16,8,128]{2,1,0:T(8,128)S(1)} all-to-all(f32[16,8,128]{2,1,0:T(8,128)S(1)} %shard_map.47), channel_id=1, replica_groups={{0,1,2,3,4,5,6,7,8,9,10,11,12,13,14,15},{16,17,18,19,20,21,22,23,24,25,..., dimensions={0} | all-to-all | bytes 131072 | tf_op jit(solution)/shard_map/all_to_all | solution.py:340
  55.0 6.2 %shard_map.48 = (f32[2048,1024]{1,0:T(8,128)}, f32[16,128]{1,0:T(8,128)}) custom-call(s32[1]{0:T(128)} %bitcast.device, f32[16,8,128]{2,1,0:T(8,128)S(1)} %all_to_all.11.received, f32[8,128]{1,0:T(8,128)S(1)} %get-tuple-element.23.own, bf16[2048,512]{1,0:T(8,128)(2,1)S(1)} %get-tuple-element.24.probs_ab, bf16[2048,512]{1,0:T(8,128)(2,1)S(1)} %get-tuple-element.25.probs_cd, ...), custom_call_target="tpu_custom_call" | custom-call | tf_op jit(solution)/shard_map/pallas_call | solution.py:241
  (2 shorter events, 0.1 us)
Async XLA Ops:
  0.6 1.0 %copy-start = (bf16[128,1024]{1,0:T(8,128)(2,1)S(1)}, bf16[128,1024]{1,0:T(8,128)(2,1)}, u32[]{:S(2)}) copy-start(bf16[128,1024]{1,0:T(8,128)(2,1)} %param.2) | copy-start | bytes 786436
  1.6 7.8 %collective-permute-start = (bf16[64,1024]{1,0:T(8,128)(2,1)S(1)}, bf16[64,1024]{1,0:T(8,128)(2,1)S(1)}, u32[]{:S(2)}, u32[]{:S(2)}) collective-permute-start(bf16[64,1024]{1,0:T(8,128)(2,1)S(1)} %constant_dynamic-slice_fusion.refs_0_), channel_id=1, source_target_pairs={{0,144},{1,145},{2,146},{3,147},{4,148},{5,149},{6,150},{7,151},{8... | collective-permute-start | bytes 393224 | tf_op jit(solution)/shard_map/ppermute | solution.py:348
  5.0 6.0 %collective-permute-start.6 = (bf16[64,1024]{1,0:T(8,128)(2,1)S(1)}, bf16[64,1024]{1,0:T(8,128)(2,1)S(1)}, u32[]{:S(2)}, u32[]{:S(2)}) collective-permute-start(bf16[64,1024]{1,0:T(8,128)(2,1)S(1)} %constant_dynamic-slice_fusion.refs_0_), channel_id=1, source_target_pairs={{0,96},{1,97},{2,98},{3,99},{4,100},{5,101},{6,102},{7,103},{8,104... | collective-permute-start | bytes 393224 | tf_op jit(solution)/shard_map/ppermute | solution.py:350
  7.7 7.6 %collective-permute-start.5 = (bf16[64,1024]{1,0:T(8,128)(2,1)S(1)}, bf16[64,1024]{1,0:T(8,128)(2,1)S(1)}, u32[]{:S(2)}, u32[]{:S(2)}) collective-permute-start(bf16[64,1024]{1,0:T(8,128)(2,1)S(1)} %constant_dynamic-slice_fusion.refs_0_), channel_id=1, source_target_pairs={{0,32},{1,33},{2,34},{3,35},{4,36},{5,37},{6,38},{7,39},{8,40},{9,... | collective-permute-start | bytes 393224 | tf_op jit(solution)/shard_map/ppermute | solution.py:350
  7.7 7.6 %collective-permute-start.4 = (bf16[64,1024]{1,0:T(8,128)(2,1)S(1)}, bf16[64,1024]{1,0:T(8,128)(2,1)S(1)}, u32[]{:S(2)}, u32[]{:S(2)}) collective-permute-start(bf16[64,1024]{1,0:T(8,128)(2,1)S(1)} %constant_dynamic-slice_fusion.refs_0_), channel_id=1, source_target_pairs={{0,64},{1,65},{2,66},{3,67},{4,68},{5,69},{6,70},{7,71},{8,72},{9,... | collective-permute-start | bytes 393224 | tf_op jit(solution)/shard_map/ppermute | solution.py:350
  9.4 11.6 %collective-permute-start.3 = (bf16[64,1024]{1,0:T(8,128)(2,1)S(1)}, bf16[64,1024]{1,0:T(8,128)(2,1)S(1)}, u32[]{:S(2)}, u32[]{:S(2)}) collective-permute-start(bf16[64,1024]{1,0:T(8,128)(2,1)S(1)} %collective-permute-done.refs_0_), channel_id=1, source_target_pairs={{0,96},{1,97},{2,98},{3,99},{4,100},{5,101},{6,102},{7,103},{8,104... | collective-permute-start | bytes 393224 | tf_op jit(solution)/shard_map/ppermute | solution.py:351
  10.8 11.1 %collective-permute-start.2 = (bf16[64,1024]{1,0:T(8,128)(2,1)S(1)}, bf16[64,1024]{1,0:T(8,128)(2,1)S(1)}, u32[]{:S(2)}, u32[]{:S(2)}) collective-permute-start(bf16[64,1024]{1,0:T(8,128)(2,1)S(1)} %collective-permute-done.refs_0_), channel_id=1, source_target_pairs={{0,32},{1,33},{2,34},{3,35},{4,36},{5,37},{6,38},{7,39},{8,40},{9,... | collective-permute-start | bytes 393224 | tf_op jit(solution)/shard_map/ppermute | solution.py:351
  11.0 11.0 %collective-permute-start.1 = (bf16[64,1024]{1,0:T(8,128)(2,1)S(1)}, bf16[64,1024]{1,0:T(8,128)(2,1)S(1)}, u32[]{:S(2)}, u32[]{:S(2)}) collective-permute-start(bf16[64,1024]{1,0:T(8,128)(2,1)S(1)} %collective-permute-done.refs_0_), channel_id=1, source_target_pairs={{0,64},{1,65},{2,66},{3,67},{4,68},{5,69},{6,70},{7,71},{8,72},{9,... | collective-permute-start | bytes 393224 | tf_op jit(solution)/shard_map/ppermute | solution.py:351
  15.4 8.2 %collective-permute-start.8 = (bf16[256,1024]{1,0:T(8,128)(2,1)S(1)}, bf16[256,1024]{1,0:T(8,128)(2,1)S(1)}, u32[]{:S(2)}, u32[]{:S(2)}) collective-permute-start(bf16[256,1024]{1,0:T(8,128)(2,1)S(1)} %shard_map.42.rows.rows_a), channel_id=1, source_target_pairs={{0,1},{1,0},{2,3},{3,2},{4,5},{5,4},{6,7},{7,6},{8,9},{9,8},{10,11... | collective-permute-start | bytes 1572872 | tf_op jit(solution)/shard_map/ppermute | solution.py:353
  22.0 4.7 %collective-permute-start.7 = (bf16[256,1024]{1,0:T(8,128)(2,1)S(1)}, bf16[256,1024]{1,0:T(8,128)(2,1)S(1)}, u32[]{:S(2)}, u32[]{:S(2)}) collective-permute-start(bf16[256,1024]{1,0:T(8,128)(2,1)S(1)} %shard_map.44.rows_b), channel_id=1, source_target_pairs={{0,1},{1,0},{2,3},{3,2},{4,5},{5,4},{6,7},{7,6},{8,9},{9,8},{10,11... | collective-permute-start | bytes 1572872 | tf_op jit(solution)/shard_map/ppermute | solution.py:356

commit v5 on v4

--- a/solution.py
+++ b/solution.py
@@ -36,7 +36,7 @@
 
 x_step = [(d, d ^ X_HI ^ X_LO) for d in range(DEVICES)]
 core_step = [(d, d ^ 1) for d in range(DEVICES)]
-Y_STEPS = (2, 1, 3)
+Y_STEPS = (2, 3, 1)
 plane_groups = groups_by(lambda d: d % X_LO)
 column_groups = groups_by(lambda d: d // X_LO)
 

time: 61.5 us -> 60.9 us (level)
  starting transfers between devices: 17 us -> 15.1 us
  blocking collectives: 26.3 us -> 27.2 us
    ppermute x1, starting transfers between devices: 4.26 us -> 2.47 us  [per_device(): rows_c = lax.ppermute(rows_a, AXES, core_step)]
    all_to_all x2, blocking collectives: 26.3 us -> 27.2 us  [to_group(): lax.all_to_all(message, AXES, 0, 0, tiled=True, axis_index_groups=groups)]
  transfers between devices with their start and end apart: 9 -> 9, of which waited for: 1 -> 1; matrix products, arithmetic and copies ran while one was open for 0% -> 0% of each run, Pallas kernels for 11% -> 12%
where the time goes in v5:
time: 60.9 us; the launch traced here: 60.7 us
  blocking collectives  27.2 us (45%)
  starting transfers between devices  15.1 us (25%)
  Pallas kernels  15.1 us (25%)
  waiting for transfers between devices  1.43 us (2%)
  local copies, waits for them, and re-layouts  0.94 us (2%)
  between operations  0.9 us (1%)
    all_to_all x2, blocking collectives, to_group(): lax.all_to_all(message, AXES, 0, 0, tiled=True, axis_index_groups=groups)  27.2 us
    pallas_call x8, Pallas kernels, call(): pl.pallas_call(kernel, out_shape=outs, in_specs=in_specs, out_specs=out_s...  15.1 us
    ppermute x3, starting transfers between devices, per_device(): near = [lax.ppermute(mine, AXES, y_step(steps)) for steps in Y_STEPS]  4.38 us
    ppermute x1, starting transfers between devices, per_device(): other = lax.ppermute(mine, AXES, x_step)  3.39 us
    ppermute x3, starting transfers between devices, per_device(): far = [lax.ppermute(other, AXES, y_step(steps)) for steps in Y_STEPS]  3.09 us
    ppermute x1, starting transfers between devices, per_device(): rows_c = lax.ppermute(rows_a, AXES, core_step)  2.47 us
    ppermute x1, starting transfers between devices, per_device(): rows_d = lax.ppermute(rows_b, AXES, core_step)  1.78 us
    ppermute x3, waiting for transfers between devices, per_device(): far = [lax.ppermute(other, AXES, y_step(steps)) for steps in Y_STEPS]  1.41 us
  transfers between devices with their start and end apart: 9, of which 1 were waited for; matrix products, arithmetic and copies ran while one was open for 0% of the time, Pallas kernels for 12%

profile of v5, /device:TPU:1, one launch (start us, length us, event | category | flops | bytes accessed | tf_op | source)
XLA Modules:
  0.0 60.7 jit_solution(868238187751544218)
XLA Ops:
  0.6 0.0 copy-start
  0.7 0.9 %copy-done = bf16[128,1024]{1,0:T(8,128)(2,1)S(1)} copy-done((bf16[128,1024]{1,0:T(8,128)(2,1)S(1)}, bf16[128,1024]{1,0:T(8,128)(2,1)}, u32[]{:S(2)}) %copy-start) | copy-done | bytes 262168
  1.6 3.4 %collective-permute-start = (bf16[64,1024]{1,0:T(8,128)(2,1)S(1)}, bf16[64,1024]{1,0:T(8,128)(2,1)S(1)}, u32[]{:S(2)}, u32[]{:S(2)}) collective-permute-start(bf16[64,1024]{1,0:T(8,128)(2,1)S(1)} %constant_dynamic-slice_fusion.refs_0_), channel_id=1, source_target_pairs={{0,144},{1,145},{2,146},{3,147},{4,148},{5,149},{6,150},{7,151},{8... | collective-permute-start | bytes 393224 | tf_op jit(solution)/shard_map/ppermute | solution.py:348
  5.0 1.3 %collective-permute-start.6 = (bf16[64,1024]{1,0:T(8,128)(2,1)S(1)}, bf16[64,1024]{1,0:T(8,128)(2,1)S(1)}, u32[]{:S(2)}, u32[]{:S(2)}) collective-permute-start(bf16[64,1024]{1,0:T(8,128)(2,1)S(1)} %constant_dynamic-slice_fusion.refs_0_), channel_id=1, source_target_pairs={{0,32},{1,33},{2,34},{3,35},{4,36},{5,37},{6,38},{7,39},{8,40},{9,... | collective-permute-start | bytes 393224 | tf_op jit(solution)/shard_map/ppermute | solution.py:350
  6.3 1.4 %collective-permute-start.5 = (bf16[64,1024]{1,0:T(8,128)(2,1)S(1)}, bf16[64,1024]{1,0:T(8,128)(2,1)S(1)}, u32[]{:S(2)}, u32[]{:S(2)}) collective-permute-start(bf16[64,1024]{1,0:T(8,128)(2,1)S(1)} %constant_dynamic-slice_fusion.refs_0_), channel_id=1, source_target_pairs={{0,96},{1,97},{2,98},{3,99},{4,100},{5,101},{6,102},{7,103},{8,104... | collective-permute-start | bytes 393224 | tf_op jit(solution)/shard_map/ppermute | solution.py:350
  7.7 1.6 %collective-permute-start.4 = (bf16[64,1024]{1,0:T(8,128)(2,1)S(1)}, bf16[64,1024]{1,0:T(8,128)(2,1)S(1)}, u32[]{:S(2)}, u32[]{:S(2)}) collective-permute-start(bf16[64,1024]{1,0:T(8,128)(2,1)S(1)} %constant_dynamic-slice_fusion.refs_0_), channel_id=1, source_target_pairs={{0,64},{1,65},{2,66},{3,67},{4,68},{5,69},{6,70},{7,71},{8,72},{9,... | collective-permute-start | bytes 393224 | tf_op jit(solution)/shard_map/ppermute | solution.py:350
  9.4 0.0 collective-permute-done.refs_0_
  9.4 0.4 collective-permute-start.3
  9.8 2.3 %collective-permute-start.2 = (bf16[64,1024]{1,0:T(8,128)(2,1)S(1)}, bf16[64,1024]{1,0:T(8,128)(2,1)S(1)}, u32[]{:S(2)}, u32[]{:S(2)}) collective-permute-start(bf16[64,1024]{1,0:T(8,128)(2,1)S(1)} %collective-permute-done.refs_0_), channel_id=1, source_target_pairs={{0,96},{1,97},{2,98},{3,99},{4,100},{5,101},{6,102},{7,103},{8,104... | collective-permute-start | bytes 393224 | tf_op jit(solution)/shard_map/ppermute | solution.py:351
  12.1 0.0 collective-permute-done.6.refs_3_
  12.1 0.4 collective-permute-start.1
  12.5 2.5 %shard_map.41 = (bf16[2048,1024]{1,0:T(8,128)(2,1)S(1)}, f32[2048,128]{1,0:T(8,128)S(1)}, f32[8,128]{1,0:T(8,128)S(1)}) custom-call(s32[1]{0:T(128)} %bitcast.device, bf16[2048,1024]{1,0:T(8,128)(2,1)} %source.1), custom_call_target="tpu_custom_call" | custom-call | tf_op jit(solution)/shard_map/pallas_call | solution.py:241
  15.0 0.0 collective-permute-done.5.refs_2_
  15.0 0.0 collective-permute-done.4.refs_1_
  15.0 0.1 shard_map.42.rows.rows_a
  15.1 2.5 %collective-permute-start.8 = (bf16[256,1024]{1,0:T(8,128)(2,1)S(1)}, bf16[256,1024]{1,0:T(8,128)(2,1)S(1)}, u32[]{:S(2)}, u32[]{:S(2)}) collective-permute-start(bf16[256,1024]{1,0:T(8,128)(2,1)S(1)} %shard_map.42.rows.rows_a), channel_id=1, source_target_pairs={{0,1},{1,0},{2,3},{3,2},{4,5},{5,4},{6,7},{7,6},{8,9},{9,8},{10,11... | collective-permute-start | bytes 1572872 | tf_op jit(solution)/shard_map/ppermute | solution.py:353
  17.5 1.3 %shard_map.43 = (f32[1,256]{1,0:T(1,128)S(1)}, f32[2048,256]{1,0:T(8,128)S(1)}) custom-call(bf16[2048,1024]{1,0:T(8,128)(2,1)S(1)} %get-tuple-element.15.cents, f32[2048,128]{1,0:T(8,128)S(1)} %get-tuple-element.16.bias, bf16[256,1024]{1,0:T(8,128)(2,1)S(1)} %shard_map.42.rows.rows_a), custom_call_target="tpu_custom_call" | custom-call | tf_op jit(solution)/shard_map/pallas_call | solution.py:241
  18.9 0.0 collective-permute-done.3.refs_3_
  18.9 0.0 collective-permute-done.2.refs_2_
  18.9 1.4 %collective-permute-done.1.refs_1_ = bf16[64,1024]{1,0:T(8,128)(2,1)S(1)} collective-permute-done((bf16[64,1024]{1,0:T(8,128)(2,1)S(1)}, bf16[64,1024]{1,0:T(8,128)(2,1)S(1)}, u32[]{:S(2)}, u32[]{:S(2)}) %collective-permute-start.1) | collective-permute-done | bytes 131104 | tf_op jit(solution)/shard_map/ppermute | solution.py:351
  20.3 1.8 %collective-permute-start.7 = (bf16[256,1024]{1,0:T(8,128)(2,1)S(1)}, bf16[256,1024]{1,0:T(8,128)(2,1)S(1)}, u32[]{:S(2)}, u32[]{:S(2)}) collective-permute-start(bf16[256,1024]{1,0:T(8,128)(2,1)S(1)} %shard_map.44.rows_b), channel_id=1, source_target_pairs={{0,1},{1,0},{2,3},{3,2},{4,5},{5,4},{6,7},{7,6},{8,9},{9,8},{10,11... | collective-permute-start | bytes 1572872 | tf_op jit(solution)/shard_map/ppermute | solution.py:356
  22.1 0.0 collective-permute-done.8.rows_c
  22.1 3.1 %shard_map.45 = (bf16[2048,512]{1,0:T(8,128)(2,1)S(1)}, f32[5,256]{1,0:T(8,128)S(1)}, f32[2048,256]{1,0:T(8,128)S(1)}) custom-call(bf16[2048,1024]{1,0:T(8,128)(2,1)S(1)} %get-tuple-element.15.cents, f32[2048,128]{1,0:T(8,128)S(1)} %get-tuple-element.16.bias, bf16[256,1024]{1,0:T(8,128)(2,1)S(1)} %shard_map.44.rows_b, ...), custom_call_target="tpu_custom_call" | custom-call | tf_op jit(solution)/shard_map/pallas_call | solution.py:241
  25.2 0.0 collective-permute-done.7.rows_d
  25.2 1.9 %shard_map.46 = (bf16[2048,512]{1,0:T(8,128)(2,1)S(1)}, f32[8,128]{1,0:T(8,128)S(1)}, f32[16,8,128]{2,1,0:T(8,128)S(1)}) custom-call(s32[1]{0:T(128)} %bitcast.device, bf16[2048,1024]{1,0:T(8,128)(2,1)S(1)} %get-tuple-element.15.cents, f32[2048,128]{1,0:T(8,128)S(1)} %get-tuple-element.16.bias, bf16[256,1024]{1,0:T(8,128)(2,1)S(1)} %collective-permute-done.7.rows_d, ...), custom_call_target="tpu_custom_call" | custom-call | tf_op jit(solution)/shard_map/pallas_call | solution.py:241
  27.2 10.3 %all_to_all.10.received = f32[16,8,128]{2,1,0:T(8,128)S(1)} all-to-all(f32[16,8,128]{2,1,0:T(8,128)S(1)} %get-tuple-element.22), channel_id=1, replica_groups={{0,16,32,48,64,80,96,112,128,144,160,176,192,208,224,240},{1,17,33,49,6..., dimensions={0} | all-to-all | bytes 131072 | tf_op jit(solution)/shard_map/all_to_all | solution.py:340
  37.4 0.1 shard_map.47
  37.5 16.9 %all_to_all.11.received = f32[16,8,128]{2,1,0:T(8,128)S(1)} all-to-all(f32[16,8,128]{2,1,0:T(8,128)S(1)} %shard_map.47), channel_id=1, replica_groups={{0,1,2,3,4,5,6,7,8,9,10,11,12,13,14,15},{16,17,18,19,20,21,22,23,24,25,..., dimensions={0} | all-to-all | bytes 131072 | tf_op jit(solution)/shard_map/all_to_all | solution.py:340
  54.4 6.2 %shard_map.48 = (f32[2048,1024]{1,0:T(8,128)}, f32[16,128]{1,0:T(8,128)}) custom-call(s32[1]{0:T(128)} %bitcast.device, f32[16,8,128]{2,1,0:T(8,128)S(1)} %all_to_all.11.received, f32[8,128]{1,0:T(8,128)S(1)} %get-tuple-element.23.own, bf16[2048,512]{1,0:T(8,128)(2,1)S(1)} %get-tuple-element.24.probs_ab, bf16[2048,512]{1,0:T(8,128)(2,1)S(1)} %get-tuple-element.25.probs_cd, ...), custom_call_target="tpu_custom_call" | custom-call | tf_op jit(solution)/shard_map/pallas_call | solution.py:241
  (2 shorter events, 0.1 us)
Async XLA Ops:
  0.6 1.0 %copy-start = (bf16[128,1024]{1,0:T(8,128)(2,1)S(1)}, bf16[128,1024]{1,0:T(8,128)(2,1)}, u32[]{:S(2)}) copy-start(bf16[128,1024]{1,0:T(8,128)(2,1)} %param.2) | copy-start | bytes 786436
  1.6 7.8 %collective-permute-start = (bf16[64,1024]{1,0:T(8,128)(2,1)S(1)}, bf16[64,1024]{1,0:T(8,128)(2,1)S(1)}, u32[]{:S(2)}, u32[]{:S(2)}) collective-permute-start(bf16[64,1024]{1,0:T(8,128)(2,1)S(1)} %constant_dynamic-slice_fusion.refs_0_), channel_id=1, source_target_pairs={{0,144},{1,145},{2,146},{3,147},{4,148},{5,149},{6,150},{7,151},{8... | collective-permute-start | bytes 393224 | tf_op jit(solution)/shard_map/ppermute | solution.py:348
  5.0 7.1 %collective-permute-start.6 = (bf16[64,1024]{1,0:T(8,128)(2,1)S(1)}, bf16[64,1024]{1,0:T(8,128)(2,1)S(1)}, u32[]{:S(2)}, u32[]{:S(2)}) collective-permute-start(bf16[64,1024]{1,0:T(8,128)(2,1)S(1)} %constant_dynamic-slice_fusion.refs_0_), channel_id=1, source_target_pairs={{0,32},{1,33},{2,34},{3,35},{4,36},{5,37},{6,38},{7,39},{8,40},{9,... | collective-permute-start | bytes 393224 | tf_op jit(solution)/shard_map/ppermute | solution.py:350
  6.3 8.7 %collective-permute-start.5 = (bf16[64,1024]{1,0:T(8,128)(2,1)S(1)}, bf16[64,1024]{1,0:T(8,128)(2,1)S(1)}, u32[]{:S(2)}, u32[]{:S(2)}) collective-permute-start(bf16[64,1024]{1,0:T(8,128)(2,1)S(1)} %constant_dynamic-slice_fusion.refs_0_), channel_id=1, source_target_pairs={{0,96},{1,97},{2,98},{3,99},{4,100},{5,101},{6,102},{7,103},{8,104... | collective-permute-start | bytes 393224 | tf_op jit(solution)/shard_map/ppermute | solution.py:350
  7.7 7.3 %collective-permute-start.4 = (bf16[64,1024]{1,0:T(8,128)(2,1)S(1)}, bf16[64,1024]{1,0:T(8,128)(2,1)S(1)}, u32[]{:S(2)}, u32[]{:S(2)}) collective-permute-start(bf16[64,1024]{1,0:T(8,128)(2,1)S(1)} %constant_dynamic-slice_fusion.refs_0_), channel_id=1, source_target_pairs={{0,64},{1,65},{2,66},{3,67},{4,68},{5,69},{6,70},{7,71},{8,72},{9,... | collective-permute-start | bytes 393224 | tf_op jit(solution)/shard_map/ppermute | solution.py:350
  9.4 9.5 %collective-permute-start.3 = (bf16[64,1024]{1,0:T(8,128)(2,1)S(1)}, bf16[64,1024]{1,0:T(8,128)(2,1)S(1)}, u32[]{:S(2)}, u32[]{:S(2)}) collective-permute-start(bf16[64,1024]{1,0:T(8,128)(2,1)S(1)} %collective-permute-done.refs_0_), channel_id=1, source_target_pairs={{0,32},{1,33},{2,34},{3,35},{4,36},{5,37},{6,38},{7,39},{8,40},{9,... | collective-permute-start | bytes 393224 | tf_op jit(solution)/shard_map/ppermute | solution.py:351
  9.8 9.1 %collective-permute-start.2 = (bf16[64,1024]{1,0:T(8,128)(2,1)S(1)}, bf16[64,1024]{1,0:T(8,128)(2,1)S(1)}, u32[]{:S(2)}, u32[]{:S(2)}) collective-permute-start(bf16[64,1024]{1,0:T(8,128)(2,1)S(1)} %collective-permute-done.refs_0_), channel_id=1, source_target_pairs={{0,96},{1,97},{2,98},{3,99},{4,100},{5,101},{6,102},{7,103},{8,104... | collective-permute-start | bytes 393224 | tf_op jit(solution)/shard_map/ppermute | solution.py:351
  12.1 8.2 %collective-permute-start.1 = (bf16[64,1024]{1,0:T(8,128)(2,1)S(1)}, bf16[64,1024]{1,0:T(8,128)(2,1)S(1)}, u32[]{:S(2)}, u32[]{:S(2)}) collective-permute-start(bf16[64,1024]{1,0:T(8,128)(2,1)S(1)} %collective-permute-done.refs_0_), channel_id=1, source_target_pairs={{0,64},{1,65},{2,66},{3,67},{4,68},{5,69},{6,70},{7,71},{8,72},{9,... | collective-permute-start | bytes 393224 | tf_op jit(solution)/shard_map/ppermute | solution.py:351
  15.1 7.1 %collective-permute-start.8 = (bf16[256,1024]{1,0:T(8,128)(2,1)S(1)}, bf16[256,1024]{1,0:T(8,128)(2,1)S(1)}, u32[]{:S(2)}, u32[]{:S(2)}) collective-permute-start(bf16[256,1024]{1,0:T(8,128)(2,1)S(1)} %shard_map.42.rows.rows_a), channel_id=1, source_target_pairs={{0,1},{1,0},{2,3},{3,2},{4,5},{5,4},{6,7},{7,6},{8,9},{9,8},{10,11... | collective-permute-start | bytes 1572872 | tf_op jit(solution)/shard_map/ppermute | solution.py:353
  20.3 4.9 %collective-permute-start.7 = (bf16[256,1024]{1,0:T(8,128)(2,1)S(1)}, bf16[256,1024]{1,0:T(8,128)(2,1)S(1)}, u32[]{:S(2)}, u32[]{:S(2)}) collective-permute-start(bf16[256,1024]{1,0:T(8,128)(2,1)S(1)} %shard_map.44.rows_b), channel_id=1, source_target_pairs={{0,1},{1,0},{2,3},{3,2},{4,5},{5,4},{6,7},{7,6},{8,9},{9,8},{10,11... | collective-permute-start | bytes 1572872 | tf_op jit(solution)/shard_map/ppermute | solution.py:356

commit v6 on v5

--- a/solution.py
+++ b/solution.py
@@ -13,7 +13,7 @@
 AXES = ("blk", "grp")
 LANES = 128
 ROW_TILE = 256
-CENT_TILE = 256
+CENT_TILE = 512
 OUT_COLS = 512
 OUT_ROWS = 256
 MIB = 1024 * 1024

time: 60.9 us -> 60.9 us (level)
  transfers between devices with their start and end apart: 9 -> 9, of which waited for: 1 -> 1; matrix products, arithmetic and copies ran while one was open for 0% -> 0% of each run, Pallas kernels for 12% -> 11%
where the time goes in v6:
time: 60.9 us; the launch traced here: 60.7 us
  blocking collectives  27.2 us (45%)
  starting transfers between devices  15.1 us (25%)
  Pallas kernels  15.1 us (25%)
  waiting for transfers between devices  1.44 us (2%)
  local copies, waits for them, and re-layouts  0.94 us (2%)
  between operations  0.9 us (1%)
    all_to_all x2, blocking collectives, to_group(): lax.all_to_all(message, AXES, 0, 0, tiled=True, axis_index_groups=groups)  27.2 us
    pallas_call x8, Pallas kernels, call(): pl.pallas_call(kernel, out_shape=outs, in_specs=in_specs, out_specs=out_s...  15.1 us
    ppermute x3, starting transfers between devices, per_device(): near = [lax.ppermute(mine, AXES, y_step(steps)) for steps in Y_STEPS]  4.38 us
    ppermute x1, starting transfers between devices, per_device(): other = lax.ppermute(mine, AXES, x_step)  3.39 us
    ppermute x3, starting transfers between devices, per_device(): far = [lax.ppermute(other, AXES, y_step(steps)) for steps in Y_STEPS]  3.09 us
    ppermute x1, starting transfers between devices, per_device(): rows_c = lax.ppermute(rows_a, AXES, core_step)  2.47 us
    ppermute x1, starting transfers between devices, per_device(): rows_d = lax.ppermute(rows_b, AXES, core_step)  1.78 us
    ppermute x3, waiting for transfers between devices, per_device(): far = [lax.ppermute(other, AXES, y_step(steps)) for steps in Y_STEPS]  1.42 us
  transfers between devices with their start and end apart: 9, of which 1 were waited for; matrix products, arithmetic and copies ran while one was open for 0% of the time, Pallas kernels for 11%

profile of v6, /device:TPU:1, one launch (start us, length us, event | category | flops | bytes accessed | tf_op | source)
XLA Modules:
  0.0 60.7 jit_solution(10582492817485472474)
XLA Ops:
  0.6 0.0 copy-start
  0.7 0.9 %copy-done = bf16[128,1024]{1,0:T(8,128)(2,1)S(1)} copy-done((bf16[128,1024]{1,0:T(8,128)(2,1)S(1)}, bf16[128,1024]{1,0:T(8,128)(2,1)}, u32[]{:S(2)}) %copy-start) | copy-done | bytes 262168
  1.6 3.4 %collective-permute-start = (bf16[64,1024]{1,0:T(8,128)(2,1)S(1)}, bf16[64,1024]{1,0:T(8,128)(2,1)S(1)}, u32[]{:S(2)}, u32[]{:S(2)}) collective-permute-start(bf16[64,1024]{1,0:T(8,128)(2,1)S(1)} %constant_dynamic-slice_fusion.refs_0_), channel_id=1, source_target_pairs={{0,144},{1,145},{2,146},{3,147},{4,148},{5,149},{6,150},{7,151},{8... | collective-permute-start | bytes 393224 | tf_op jit(solution)/shard_map/ppermute | solution.py:348
  5.0 1.3 %collective-permute-start.6 = (bf16[64,1024]{1,0:T(8,128)(2,1)S(1)}, bf16[64,1024]{1,0:T(8,128)(2,1)S(1)}, u32[]{:S(2)}, u32[]{:S(2)}) collective-permute-start(bf16[64,1024]{1,0:T(8,128)(2,1)S(1)} %constant_dynamic-slice_fusion.refs_0_), channel_id=1, source_target_pairs={{0,32},{1,33},{2,34},{3,35},{4,36},{5,37},{6,38},{7,39},{8,40},{9,... | collective-permute-start | bytes 393224 | tf_op jit(solution)/shard_map/ppermute | solution.py:350
  6.3 1.4 %collective-permute-start.5 = (bf16[64,1024]{1,0:T(8,128)(2,1)S(1)}, bf16[64,1024]{1,0:T(8,128)(2,1)S(1)}, u32[]{:S(2)}, u32[]{:S(2)}) collective-permute-start(bf16[64,1024]{1,0:T(8,128)(2,1)S(1)} %constant_dynamic-slice_fusion.refs_0_), channel_id=1, source_target_pairs={{0,96},{1,97},{2,98},{3,99},{4,100},{5,101},{6,102},{7,103},{8,104... | collective-permute-start | bytes 393224 | tf_op jit(solution)/shard_map/ppermute | solution.py:350
  7.7 1.6 %collective-permute-start.4 = (bf16[64,1024]{1,0:T(8,128)(2,1)S(1)}, bf16[64,1024]{1,0:T(8,128)(2,1)S(1)}, u32[]{:S(2)}, u32[]{:S(2)}) collective-permute-start(bf16[64,1024]{1,0:T(8,128)(2,1)S(1)} %constant_dynamic-slice_fusion.refs_0_), channel_id=1, source_target_pairs={{0,64},{1,65},{2,66},{3,67},{4,68},{5,69},{6,70},{7,71},{8,72},{9,... | collective-permute-start | bytes 393224 | tf_op jit(solution)/shard_map/ppermute | solution.py:350
  9.4 0.0 collective-permute-done.refs_0_
  9.4 0.4 collective-permute-start.3
  9.8 2.3 %collective-permute-start.2 = (bf16[64,1024]{1,0:T(8,128)(2,1)S(1)}, bf16[64,1024]{1,0:T(8,128)(2,1)S(1)}, u32[]{:S(2)}, u32[]{:S(2)}) collective-permute-start(bf16[64,1024]{1,0:T(8,128)(2,1)S(1)} %collective-permute-done.refs_0_), channel_id=1, source_target_pairs={{0,96},{1,97},{2,98},{3,99},{4,100},{5,101},{6,102},{7,103},{8,104... | collective-permute-start | bytes 393224 | tf_op jit(solution)/shard_map/ppermute | solution.py:351
  12.1 0.0 collective-permute-done.6.refs_3_
  12.1 0.4 collective-permute-start.1
  12.5 2.5 %shard_map.41 = (bf16[2048,1024]{1,0:T(8,128)(2,1)S(1)}, f32[2048,128]{1,0:T(8,128)S(1)}, f32[8,128]{1,0:T(8,128)S(1)}) custom-call(s32[1]{0:T(128)} %bitcast.device, bf16[2048,1024]{1,0:T(8,128)(2,1)} %source.1), custom_call_target="tpu_custom_call" | custom-call | tf_op jit(solution)/shard_map/pallas_call | solution.py:241
  15.0 0.0 collective-permute-done.5.refs_2_
  15.0 0.0 collective-permute-done.4.refs_1_
  15.0 0.1 shard_map.42.rows.rows_a
  15.1 2.5 %collective-permute-start.8 = (bf16[256,1024]{1,0:T(8,128)(2,1)S(1)}, bf16[256,1024]{1,0:T(8,128)(2,1)S(1)}, u32[]{:S(2)}, u32[]{:S(2)}) collective-permute-start(bf16[256,1024]{1,0:T(8,128)(2,1)S(1)} %shard_map.42.rows.rows_a), channel_id=1, source_target_pairs={{0,1},{1,0},{2,3},{3,2},{4,5},{5,4},{6,7},{7,6},{8,9},{9,8},{10,11... | collective-permute-start | bytes 1572872 | tf_op jit(solution)/shard_map/ppermute | solution.py:353
  17.5 1.3 %shard_map.43 = (f32[1,256]{1,0:T(1,128)S(1)}, f32[2048,256]{1,0:T(8,128)S(1)}) custom-call(bf16[2048,1024]{1,0:T(8,128)(2,1)S(1)} %get-tuple-element.15.cents, f32[2048,128]{1,0:T(8,128)S(1)} %get-tuple-element.16.bias, bf16[256,1024]{1,0:T(8,128)(2,1)S(1)} %shard_map.42.rows.rows_a), custom_call_target="tpu_custom_call" | custom-call | tf_op jit(solution)/shard_map/pallas_call | solution.py:241
  18.8 0.0 collective-permute-done.3.refs_3_
  18.9 0.0 collective-permute-done.2.refs_2_
  18.9 1.4 %collective-permute-done.1.refs_1_ = bf16[64,1024]{1,0:T(8,128)(2,1)S(1)} collective-permute-done((bf16[64,1024]{1,0:T(8,128)(2,1)S(1)}, bf16[64,1024]{1,0:T(8,128)(2,1)S(1)}, u32[]{:S(2)}, u32[]{:S(2)}) %collective-permute-start.1) | collective-permute-done | bytes 131104 | tf_op jit(solution)/shard_map/ppermute | solution.py:351
  20.3 1.8 %collective-permute-start.7 = (bf16[256,1024]{1,0:T(8,128)(2,1)S(1)}, bf16[256,1024]{1,0:T(8,128)(2,1)S(1)}, u32[]{:S(2)}, u32[]{:S(2)}) collective-permute-start(bf16[256,1024]{1,0:T(8,128)(2,1)S(1)} %shard_map.44.rows_b), channel_id=1, source_target_pairs={{0,1},{1,0},{2,3},{3,2},{4,5},{5,4},{6,7},{7,6},{8,9},{9,8},{10,11... | collective-permute-start | bytes 1572872 | tf_op jit(solution)/shard_map/ppermute | solution.py:356
  22.1 0.0 collective-permute-done.8.rows_c
  22.1 3.1 %shard_map.45 = (bf16[2048,512]{1,0:T(8,128)(2,1)S(1)}, f32[5,256]{1,0:T(8,128)S(1)}, f32[2048,256]{1,0:T(8,128)S(1)}) custom-call(bf16[2048,1024]{1,0:T(8,128)(2,1)S(1)} %get-tuple-element.15.cents, f32[2048,128]{1,0:T(8,128)S(1)} %get-tuple-element.16.bias, bf16[256,1024]{1,0:T(8,128)(2,1)S(1)} %shard_map.44.rows_b, ...), custom_call_target="tpu_custom_call" | custom-call | tf_op jit(solution)/shard_map/pallas_call | solution.py:241
  25.2 0.0 collective-permute-done.7.rows_d
  25.2 2.0 %shard_map.46 = (bf16[2048,512]{1,0:T(8,128)(2,1)S(1)}, f32[8,128]{1,0:T(8,128)S(1)}, f32[16,8,128]{2,1,0:T(8,128)S(1)}) custom-call(s32[1]{0:T(128)} %bitcast.device, bf16[2048,1024]{1,0:T(8,128)(2,1)S(1)} %get-tuple-element.15.cents, f32[2048,128]{1,0:T(8,128)S(1)} %get-tuple-element.16.bias, bf16[256,1024]{1,0:T(8,128)(2,1)S(1)} %collective-permute-done.7.rows_d, ...), custom_call_target="tpu_custom_call" | custom-call | tf_op jit(solution)/shard_map/pallas_call | solution.py:241
  27.2 10.3 %all_to_all.10.received = f32[16,8,128]{2,1,0:T(8,128)S(1)} all-to-all(f32[16,8,128]{2,1,0:T(8,128)S(1)} %get-tuple-element.22), channel_id=1, replica_groups={{0,16,32,48,64,80,96,112,128,144,160,176,192,208,224,240},{1,17,33,49,6..., dimensions={0} | all-to-all | bytes 131072 | tf_op jit(solution)/shard_map/all_to_all | solution.py:340
  37.4 0.1 shard_map.47
  37.5 16.9 %all_to_all.11.received = f32[16,8,128]{2,1,0:T(8,128)S(1)} all-to-all(f32[16,8,128]{2,1,0:T(8,128)S(1)} %shard_map.47), channel_id=1, replica_groups={{0,1,2,3,4,5,6,7,8,9,10,11,12,13,14,15},{16,17,18,19,20,21,22,23,24,25,..., dimensions={0} | all-to-all | bytes 131072 | tf_op jit(solution)/shard_map/all_to_all | solution.py:340
  54.4 6.2 %shard_map.48 = (f32[2048,1024]{1,0:T(8,128)}, f32[16,128]{1,0:T(8,128)}) custom-call(s32[1]{0:T(128)} %bitcast.device, f32[16,8,128]{2,1,0:T(8,128)S(1)} %all_to_all.11.received, f32[8,128]{1,0:T(8,128)S(1)} %get-tuple-element.23.own, bf16[2048,512]{1,0:T(8,128)(2,1)S(1)} %get-tuple-element.24.probs_ab, bf16[2048,512]{1,0:T(8,128)(2,1)S(1)} %get-tuple-element.25.probs_cd, ...), custom_call_target="tpu_custom_call" | custom-call | tf_op jit(solution)/shard_map/pallas_call | solution.py:241
  (2 shorter events, 0.1 us)
Async XLA Ops:
  0.6 1.0 %copy-start = (bf16[128,1024]{1,0:T(8,128)(2,1)S(1)}, bf16[128,1024]{1,0:T(8,128)(2,1)}, u32[]{:S(2)}) copy-start(bf16[128,1024]{1,0:T(8,128)(2,1)} %param.2) | copy-start | bytes 786436
  1.6 7.8 %collective-permute-start = (bf16[64,1024]{1,0:T(8,128)(2,1)S(1)}, bf16[64,1024]{1,0:T(8,128)(2,1)S(1)}, u32[]{:S(2)}, u32[]{:S(2)}) collective-permute-start(bf16[64,1024]{1,0:T(8,128)(2,1)S(1)} %constant_dynamic-slice_fusion.refs_0_), channel_id=1, source_target_pairs={{0,144},{1,145},{2,146},{3,147},{4,148},{5,149},{6,150},{7,151},{8... | collective-permute-start | bytes 393224 | tf_op jit(solution)/shard_map/ppermute | solution.py:348
  5.0 7.1 %collective-permute-start.6 = (bf16[64,1024]{1,0:T(8,128)(2,1)S(1)}, bf16[64,1024]{1,0:T(8,128)(2,1)S(1)}, u32[]{:S(2)}, u32[]{:S(2)}) collective-permute-start(bf16[64,1024]{1,0:T(8,128)(2,1)S(1)} %constant_dynamic-slice_fusion.refs_0_), channel_id=1, source_target_pairs={{0,32},{1,33},{2,34},{3,35},{4,36},{5,37},{6,38},{7,39},{8,40},{9,... | collective-permute-start | bytes 393224 | tf_op jit(solution)/shard_map/ppermute | solution.py:350
  6.3 8.7 %collective-permute-start.5 = (bf16[64,1024]{1,0:T(8,128)(2,1)S(1)}, bf16[64,1024]{1,0:T(8,128)(2,1)S(1)}, u32[]{:S(2)}, u32[]{:S(2)}) collective-permute-start(bf16[64,1024]{1,0:T(8,128)(2,1)S(1)} %constant_dynamic-slice_fusion.refs_0_), channel_id=1, source_target_pairs={{0,96},{1,97},{2,98},{3,99},{4,100},{5,101},{6,102},{7,103},{8,104... | collective-permute-start | bytes 393224 | tf_op jit(solution)/shard_map/ppermute | solution.py:350
  7.7 7.3 %collective-permute-start.4 = (bf16[64,1024]{1,0:T(8,128)(2,1)S(1)}, bf16[64,1024]{1,0:T(8,128)(2,1)S(1)}, u32[]{:S(2)}, u32[]{:S(2)}) collective-permute-start(bf16[64,1024]{1,0:T(8,128)(2,1)S(1)} %constant_dynamic-slice_fusion.refs_0_), channel_id=1, source_target_pairs={{0,64},{1,65},{2,66},{3,67},{4,68},{5,69},{6,70},{7,71},{8,72},{9,... | collective-permute-start | bytes 393224 | tf_op jit(solution)/shard_map/ppermute | solution.py:350
  9.4 9.5 %collective-permute-start.3 = (bf16[64,1024]{1,0:T(8,128)(2,1)S(1)}, bf16[64,1024]{1,0:T(8,128)(2,1)S(1)}, u32[]{:S(2)}, u32[]{:S(2)}) collective-permute-start(bf16[64,1024]{1,0:T(8,128)(2,1)S(1)} %collective-permute-done.refs_0_), channel_id=1, source_target_pairs={{0,32},{1,33},{2,34},{3,35},{4,36},{5,37},{6,38},{7,39},{8,40},{9,... | collective-permute-start | bytes 393224 | tf_op jit(solution)/shard_map/ppermute | solution.py:351
  9.8 9.1 %collective-permute-start.2 = (bf16[64,1024]{1,0:T(8,128)(2,1)S(1)}, bf16[64,1024]{1,0:T(8,128)(2,1)S(1)}, u32[]{:S(2)}, u32[]{:S(2)}) collective-permute-start(bf16[64,1024]{1,0:T(8,128)(2,1)S(1)} %collective-permute-done.refs_0_), channel_id=1, source_target_pairs={{0,96},{1,97},{2,98},{3,99},{4,100},{5,101},{6,102},{7,103},{8,104... | collective-permute-start | bytes 393224 | tf_op jit(solution)/shard_map/ppermute | solution.py:351
  12.1 8.2 %collective-permute-start.1 = (bf16[64,1024]{1,0:T(8,128)(2,1)S(1)}, bf16[64,1024]{1,0:T(8,128)(2,1)S(1)}, u32[]{:S(2)}, u32[]{:S(2)}) collective-permute-start(bf16[64,1024]{1,0:T(8,128)(2,1)S(1)} %collective-permute-done.refs_0_), channel_id=1, source_target_pairs={{0,64},{1,65},{2,66},{3,67},{4,68},{5,69},{6,70},{7,71},{8,72},{9,... | collective-permute-start | bytes 393224 | tf_op jit(solution)/shard_map/ppermute | solution.py:351
  15.1 7.1 %collective-permute-start.8 = (bf16[256,1024]{1,0:T(8,128)(2,1)S(1)}, bf16[256,1024]{1,0:T(8,128)(2,1)S(1)}, u32[]{:S(2)}, u32[]{:S(2)}) collective-permute-start(bf16[256,1024]{1,0:T(8,128)(2,1)S(1)} %shard_map.42.rows.rows_a), channel_id=1, source_target_pairs={{0,1},{1,0},{2,3},{3,2},{4,5},{5,4},{6,7},{7,6},{8,9},{9,8},{10,11... | collective-permute-start | bytes 1572872 | tf_op jit(solution)/shard_map/ppermute | solution.py:353
  20.3 4.8 %collective-permute-start.7 = (bf16[256,1024]{1,0:T(8,128)(2,1)S(1)}, bf16[256,1024]{1,0:T(8,128)(2,1)S(1)}, u32[]{:S(2)}, u32[]{:S(2)}) collective-permute-start(bf16[256,1024]{1,0:T(8,128)(2,1)S(1)} %shard_map.44.rows_b), channel_id=1, source_target_pairs={{0,1},{1,0},{2,3},{3,2},{4,5},{5,4},{6,7},{7,6},{8,9},{9,8},{10,11... | collective-permute-start | bytes 1572872 | tf_op jit(solution)/shard_map/ppermute | solution.py:356
